TPU v7x, 128 devices: a whole 4x4x4 slice. The times are simulated.
128 devices in a mesh: tm: 32 (over x, y_hi, z), space: 4 (over y_lo, core).
Axes of the slice: x: 4, y: 4 (y_hi: 2, y_lo: 2; y = y_hi * 2 + y_lo), z: 4, core: 2. Of those that a mesh axis runs over, the one named last changes fastest.
Arguments:
- video: bfloat16 [64, 32, 32, 384], P('tm', 'space'), may hold values from -6 to 6
- conv_weight: bfloat16 [3, 3, 3, 384, 384], replicated, may hold values from -0.0625 to 0.0625
- embed_weight: bfloat16 [384, 1152], replicated, may hold values from -0.3125 to 0.3125
- q_weight: bfloat16 [1152, 1152], replicated, may hold values from -0.1875 to 0.1875
- k_weight: bfloat16 [1152, 1152], replicated, may hold values from -0.1875 to 0.1875
- v_weight: bfloat16 [1152, 1152], replicated, may hold values from -0.1875 to 0.1875
- initial_state: float32 [16, 72, 72], P('space'), may hold values from -6144 to 6144
- probe_in: int32 [64, 32, 32, 1152], P('tm', 'space'), may hold values from -1 to 1, as said below
- probe_out: int32 [64, 32, 32, 1152], P('tm', None, None, 'space'), may hold values from -1 to 1, as said below
Outputs:
- flow: bfloat16 [64, 32, 32, 1152], P('tm', None, None, 'space')
- tangent: bfloat16 [64, 32, 32, 1152], P('tm', None, None, 'space')
- adjoint: bfloat16 [64, 32, 32, 1152], P('tm', 'space')
- state_cotangent: float32 [256, 16, 72, 72], P('tm', 'space')
Inputs may be any that keep to these rules, and one draw needn't show every extreme that they name: `probe_in`: every entry is -1 or +1. `probe_out`: every entry is -1 or +1.
All inputs are finite; a program needn't handle non-finite values.
Results may differ from a plain program's by a relative error of at most 0.012.
Values may be sent and summed in bfloat16 or wider, within the bound.
A program may use at most 128 MiB of HBM per device.

v0:
```python
import functools

import jax
import jax.numpy as jnp
from jax import lax
from jax.experimental import pallas as pl
from jax.experimental.pallas import tpu as pltpu
from jax.sharding import PartitionSpec as P

MESH = pl.DeviceIdType.MESH
F32 = jnp.float32
BF16 = jnp.bfloat16
D = 1152
HEADS = 16
HD = 72
C = 384
TOK = 256
TILES = D // 128
WINDOWS = (
    (0, (0, 1, 2)),
    (1, (3, 4)),
    (2, (5, 6)),
    (3, (7,)),
    (4, (8, 9)),
    (5, (10, 11)),
    (6, (12, 13)),
    (7, (14, 15)),
)
VMEM_LIMIT = 60 * 1024 * 1024


PACK = 2 * TOK + TOK // 4


def vmem():
    return pl.BlockSpec(memory_space=pltpu.VMEM)


def anywhere():
    return pl.BlockSpec(memory_space=pl.ANY)


def dot(a, b, dims=((1,), (0,))):
    return lax.dot_general(a, b, (dims, ((), ())), preferred_element_type=F32)


def head_mask(h, tile, rows):
    lane = lax.broadcasted_iota(jnp.int32, (rows, 128), 1) + 128 * tile
    return (lane >= HD * h) & (lane < HD * (h + 1))


def compact_add(tiles, t, heads, g):
    for half in range(2):
        j = t + half
        for h in heads:
            if HD * h < 128 * (j + 1) and HD * (h + 1) > 128 * j:
                r = HD * h - 128 * t
                piece = g[r : r + HD, 128 * half : 128 * half + 128]
                piece = jnp.where(head_mask(h, j, HD), piece, 0.0)
                tiles[j] = piece if tiles[j] is None else tiles[j] + piece


def block_diagonal(tiles, t, heads):
    halves = []
    for half in range(2):
        j = t + half
        parts = []
        at = 0
        for h in heads:
            r = HD * h - 128 * t
            if r > at:
                parts.append(jnp.zeros((r - at, 128), F32))
            if HD * h < 128 * (j + 1) and HD * (h + 1) > 128 * j:
                parts.append(jnp.where(head_mask(h, j, HD), tiles[j], 0.0))
            else:
                parts.append(jnp.zeros((HD, 128), F32))
            at = r + HD
        if at < 256:
            parts.append(jnp.zeros((256 - at, 128), F32))
        halves.append(jnp.concatenate(parts, 0))
    return jnp.concatenate(halves, 1).astype(BF16)


def same_head(t, heads):
    row = lax.broadcasted_iota(jnp.int32, (256, 256), 0) + 128 * t
    col = lax.broadcasted_iota(jnp.int32, (256, 256), 1) + 128 * t
    ok = None
    for h in heads:
        low, high = HD * h, HD * (h + 1)
        both = (row >= low) & (row < high) & (col >= low) & (col < high)
        ok = both if ok is None else ok | both
    return jnp.where(ok, 1.0, 0.0).astype(BF16)


def window_out(ref, f, t, value):
    if t == 0:
        ref[f, :, 0:256] = value
    else:
        ref[f, :, 128 * t : 128 * t + 128] = ref[f, :, 128 * t : 128 * t + 128] + value[:, :128]
        ref[f, :, 128 * t + 128 : 128 * t + 256] = value[:, 128:]


def pack(x):
    rest = x[:, 256:]
    rest = jnp.concatenate([rest[64 * i : 64 * i + 64] for i in range(4)], 1)
    return jnp.concatenate([x[:, :128], x[:, 128:256], rest], 0)


def unpack(x):
    rest = jnp.concatenate([x[2 * TOK :, 32 * i : 32 * i + 32] for i in range(4)], 0)
    return jnp.concatenate([x[:TOK], x[TOK : 2 * TOK], rest], 1)


def arrived(ref, sem):
    pltpu.make_async_copy(ref, ref, sem).wait()


def window(ref, f, t):
    return ref[f, :, 128 * t : 128 * t + 256]


class Scan:
    def __init__(self, place, reverse, blocks, out, got, sums, answer, totals, total, s1, r1, s2, r2, s3, r3):
        self.place, self.reverse = place, reverse
        self.blocks, self.out, self.got, self.sums, self.answer = blocks, out, got, sums, answer
        self.totals, self.total = totals, total
        self.s1, self.r1, self.s2, self.r2, self.s3, self.r3 = s1, r1, s2, r2, s3, r3
        self.share = got.shape[2]

    def rows(self, p):
        return pl.ds(pl.multiple_of(p * self.share, self.share), self.share)

    def first(self, k):
        p, device = self.place.peer(k)
        return pltpu.make_async_remote_copy(
            src_ref=self.blocks.at[:, self.rows(p)],
            dst_ref=self.got.at[self.place.me],
            send_sem=self.s1.at[p],
            recv_sem=self.r1.at[self.place.me],
            device_id=device,
            device_id_type=MESH,
        )

    def second(self, k):
        g, device = self.place.other(k)
        return pltpu.make_async_remote_copy(
            src_ref=self.total,
            dst_ref=self.totals.at[self.place.group],
            send_sem=self.s2.at[g],
            recv_sem=self.r2.at[self.place.group],
            device_id=device,
            device_id_type=MESH,
        )

    def third(self, k):
        p, device = self.place.peer(k)
        return pltpu.make_async_remote_copy(
            src_ref=self.answer.at[p],
            dst_ref=self.out.at[:, self.rows(self.place.me)],
            send_sem=self.s3.at[p],
            recv_sem=self.r3.at[self.place.me],
            device_id=device,
            device_id_type=MESH,
        )

    def start(self):
        @pl.loop(1, self.place.peers)
        def _(k):
            self.first(k).start()

        self.got[self.place.me] = self.blocks[:, self.rows(self.place.me)]

    def group_sums(self):
        @pl.loop(1, self.place.peers)
        def _(k):
            p, _ = self.place.peer(k)
            arrived(self.got.at[p], self.r1.at[p])

        nsp = self.place.nsp
        running = jnp.zeros((self.share, 128), F32)
        order = [(zz * nsp + s, f) for zz in range(self.place.nz) for f in range(2) for s in range(nsp)]
        for p, f in reversed(order) if self.reverse else order:
            running = running + self.got[p, f].astype(F32)
            self.sums[p, f] = running
        self.total[...] = running.astype(BF16)

        @pl.loop(1, self.place.groups)
        def _(k):
            self.second(k).start()

        self.totals[self.place.group] = jnp.zeros((self.share, 128), BF16)

    def send_back(self):
        @pl.loop(1, self.place.groups)
        def _(k):
            g, _ = self.place.other(k)
            arrived(self.totals.at[g], self.r2.at[g])

        group = self.place.group
        before = jnp.zeros((self.share, 128), F32)
        for g in range(self.place.groups):
            counts = g > group if self.reverse else g < group
            before = before + jnp.where(counts, self.totals[g].astype(F32), 0.0)
        for p in range(self.place.peers):
            self.answer[p] = (self.sums[p] + before[None]).astype(BF16)

        @pl.loop(1, self.place.peers)
        def _(k):
            self.third(k).start()

        self.out[:, self.rows(self.place.me)] = self.answer[self.place.me]

    def finish(self):
        @pl.loop(1, self.place.peers)
        def _(k):
            p, _ = self.place.peer(k)
            arrived(self.answer.at[p], self.r3.at[p])

    def drain(self):
        @pl.loop(1, self.place.peers)
        def _(k):
            self.first(k).wait_send()
            self.third(k).wait_send()

        @pl.loop(1, self.place.groups)
        def _(k):
            self.second(k).wait_send()


class Place:
    def __init__(self, ntm, nsp):
        self.ntm, self.nsp = ntm, nsp
        self.nz = min(4, ntm)
        self.tm, self.sp = lax.axis_index("tm"), lax.axis_index("space")
        self.peers, self.groups = self.nz * nsp, ntm // self.nz
        self.group, self.z = self.tm // self.nz, self.tm % self.nz
        self.me = self.z * nsp + self.sp

    def peer(self, k):
        p = lax.rem(self.me + k, self.peers)
        return p, (self.group * self.nz + p // self.nsp, p % self.nsp)

    def other(self, k):
        g = lax.rem(self.group + k, self.groups)
        return g, (g * self.nz + self.z, self.sp)

    def mate(self, k):
        s = lax.rem(self.sp + k, self.nsp)
        return s, (self.tm, s)


def scan_scratch(place_shape, share):
    ntm, nsp = place_shape
    nz = min(4, ntm)
    peers, groups = nz * nsp, ntm // nz
    dma = pltpu.SemaphoreType.DMA
    return [
        pltpu.VMEM((2, peers * share, 128), BF16),
        pltpu.VMEM((2, peers * share, 128), BF16),
        pltpu.VMEM((peers, 2, share, 128), BF16),
        pltpu.VMEM((peers, 2, share, 128), F32),
        pltpu.VMEM((peers, 2, share, 128), BF16),
        pltpu.VMEM((groups, share, 128), BF16),
        pltpu.VMEM((share, 128), BF16),
        dma((peers,)),
        dma((peers,)),
        dma((groups,)),
        dma((groups,)),
        dma((peers,)),
        dma((peers,)),
    ]


def exchange(place, send, recv, send_sem, recv_sem, k):
    s, device = place.mate(k)
    return pltpu.make_async_remote_copy(
        src_ref=send.at[s],
        dst_ref=recv.at[place.sp],
        send_sem=send_sem.at[s],
        recv_sem=recv_sem.at[place.sp],
        device_id=device,
        device_id_type=MESH,
    )


def kernel(
    shape,
    video, conv_h, embed_h, q_h, k_h, v_h, init_in, probe_h, po_h,
    flow_out, tangent_out, adj_out, cot_out,
    slab, q_w, k_w, v_w, q, qd, k, v, latent, po_send, po_recv, po, init_send, init_recv, init,
    out_send, out_recv, cot_send, cot_recv,
    halo_send, halo_recv, load, keep_sem, po_s, po_r, init_s, init_r, out_s, out_r, cot_s, cot_r,
    *scans,
):
    ntm, nsp = shape
    place = Place(ntm, nsp)
    tm, sp = place.tm, place.sp
    forward = Scan(place, False, *scans[: len(scans) // 2])
    backward = Scan(place, True, *scans[len(scans) // 2 :])

    later, earlier = tm + 1 < ntm, tm > 0
    down, up = sp + 1 < nsp, sp > 0
    last, first = pl.ds(TOK - 32, 32), pl.ds(0, 32)
    top, mid, bottom = pl.ds(0, 32), pl.ds(32, TOK), pl.ds(32 + TOK, 32)
    whole = pl.ds(0, TOK)
    prev, own = pl.ds(0, 2), pl.ds(2, 2)
    moves = (
        (down, up, last, own, top, (tm, sp + 1), (tm, sp - 1)),
        (up, down, first, own, bottom, (tm, sp - 1), (tm, sp + 1)),
        (later, earlier, whole, prev, mid, (tm + 1, sp), (tm - 1, sp)),
        (down & later, up & earlier, last, prev, top, (tm + 1, sp + 1), (tm - 1, sp - 1)),
        (up & later, down & earlier, first, prev, bottom, (tm + 1, sp - 1), (tm - 1, sp + 1)),
    )

    barrier = pltpu.get_barrier_semaphore()
    for _, may_recv, _, _, _, _, source in moves:

        @pl.when(may_recv)
        def _():
            pl.semaphore_signal(barrier, inc=1, device_id=source, device_id_type=MESH)

    @pl.loop(1, place.peers)
    def _(i):
        pl.semaphore_signal(barrier, inc=1, device_id=place.peer(i)[1], device_id_type=MESH)

    @pl.loop(1, place.groups)
    def _(i):
        pl.semaphore_signal(barrier, inc=1, device_id=place.other(i)[1], device_id_type=MESH)

    def encode(conv_w, embed_w, probe, po_i, taps, acc, kd, vd):
        loads = [
            pltpu.make_async_copy(src, dst, load.at[i])
            for i, (src, dst) in enumerate(
                (
                    (po_h, po_i),
                    (probe_h, probe),
                    (k_h, k_w),
                    (v_h, v_w),
                    (conv_h, conv_w),
                    (embed_h, embed_w),
                    (q_h, q_w),
                )
            )
        ]
        keep = pltpu.make_async_copy(video, slab.at[own, mid], keep_sem)
        keep.start()
        for one in loads:
            one.start()

        for _, may_recv, _, frames, there, _, _ in moves:

            @pl.when(jnp.logical_not(may_recv))
            def _():
                slab[frames, there] = jnp.zeros((2, there.size, C), BF16)

        heads = [init_in[j] for j in range(4)]
        init_send[...] = jnp.concatenate(heads + [jnp.zeros((HD, 96), F32)], 1)

        pl.semaphore_wait(barrier, sum(m[0].astype(jnp.int32) for m in moves) + place.peers + place.groups - 2)

        copies = []
        for i, (may_send, _, rows, frames, there, target, _) in enumerate(moves):
            copy = pltpu.make_async_remote_copy(
                src_ref=video.at[:, rows],
                dst_ref=slab.at[frames, there],
                send_sem=halo_send.at[i],
                recv_sem=halo_recv.at[i],
                device_id=target,
                device_id_type=MESH,
            )
            copies.append(copy)

            @pl.when(may_send)
            def _():
                copy.start()

        loads[0].wait()
        for f in range(2):
            for s in range(nsp):
                po_send[s, f] = pack(po_i[f, TOK * s : TOK * s + TOK, :].astype(F32)).astype(BF16)

        @pl.loop(1, nsp)
        def _(i):
            exchange(place, po_send, po_recv, po_s, po_r, i).start()

        po_recv[sp] = po_send[sp]

        @pl.loop(1, nsp)
        def _(i):
            init_move(i).start()

        init_recv[sp] = init_send[...]

        loads[1].wait()
        direction = probe[...].astype(F32).astype(BF16)
        for one, weight, out in zip(loads[2:4], (k_w, v_w), (kd, vd)):
            one.wait()
            out[...] = dot(direction, weight[...]).astype(BF16).reshape(2, TOK, D)

        def halo_wait(i):
            @pl.when(moves[i][1])
            def _():
                copies[i].wait_recv()

        col = lax.broadcasted_iota(jnp.int32, (TOK + 64, C), 0) % 32

        def build(f):
            here = slab[f].astype(F32)
            left = jnp.where(col == 0, 0.0, pltpu.roll(here, 1, 0))
            right = jnp.where(col == 31, 0.0, pltpu.roll(here, TOK + 63, 0))
            taps[f, :, 0:C] = left.astype(BF16)
            taps[f, :, C : 2 * C] = slab[f]
            taps[f, :, 2 * C : 3 * C] = right.astype(BF16)

        def convolve(low, high):
            @pl.loop(low, high)
            def _(tap):
                a, b = tap // 3, tap % 3
                rows = pl.ds(pl.multiple_of(b * 32, 32), TOK)
                x = taps[pl.ds(a, 2), rows, :].reshape(2 * TOK, 3 * C)
                acc[...] += dot(x, conv_w[tap])

        acc[...] = jnp.zeros_like(acc)
        keep.wait()
        halo_wait(0)
        halo_wait(1)
        build(2)
        build(3)
        loads[4].wait()
        convolve(6, 9)
        halo_wait(2)
        halo_wait(3)
        halo_wait(4)
        build(0)
        build(1)
        convolve(0, 6)

        u = acc[...]
        active = (u / (1.0 + jnp.exp(-u))).astype(BF16)
        loads[5].wait()
        latent[...] = dot(active, embed_w[...]).astype(BF16)
        for weight, out in zip((k_w, v_w), (k, v)):
            out[...] = dot(latent[...], weight[...]).astype(BF16).reshape(2, TOK, D)

        blocks = forward.blocks
        blocks[:, TILES * 144 :, :] = jnp.zeros((2, blocks.shape[1] - TILES * 144, 128), BF16)

        @pl.loop(0, 2)
        def _(f):
            st, sd = [None] * TILES, [None] * TILES
            over = ((0,), (0,))
            for t, heads in WINDOWS:
                kw, vw = window(k, f, t), window(v, f, t)
                compact_add(st, t, heads, dot(kw, vw, over))
                both = dot(window(kd, f, t), vw, over) + dot(kw, window(vd, f, t), over)
                compact_add(sd, t, heads, both)
            for j in range(TILES):
                blocks[f, 144 * j : 144 * j + 144, :] = jnp.concatenate([st[j], sd[j]], 0).astype(BF16)

        forward.start()
        loads[6].wait()
        q[...] = dot(latent[...], q_w[...]).astype(BF16).reshape(2, TOK, D)
        qd[...] = dot(direction, q_w[...]).astype(BF16).reshape(2, TOK, D)
        for copy, (may_send, *_) in zip(copies, moves):

            @pl.when(may_send)
            def _():
                copy.wait_send()

    def init_move(i):
        _, device = place.mate(i)
        return pltpu.make_async_remote_copy(
            src_ref=init_send,
            dst_ref=init_recv.at[sp],
            send_sem=init_s.at[i],
            recv_sem=init_r.at[sp],
            device_id=device,
            device_id_type=MESH,
        )

    pl.run_scoped(
        encode,
        pltpu.VMEM((9, 3 * C, C), BF16),
        pltpu.VMEM((C, D), BF16),
        pltpu.VMEM((2 * TOK, D), jnp.int32),
        pltpu.VMEM((2, 4 * TOK, D // 4), jnp.int32),
        pltpu.VMEM((4, TOK + 64, 3 * C), BF16),
        pltpu.VMEM((2 * TOK, C), F32),
        pltpu.VMEM((2, TOK, D), BF16),
        pltpu.VMEM((2, TOK, D), BF16),
    )

    forward.group_sums()

    @pl.loop(1, nsp)
    def _(i):
        s, _ = place.mate(i)
        arrived(po_recv.at[s], po_r.at[s])
        arrived(init_recv.at[s], init_r.at[s])

    for s in range(nsp):
        init[:, 288 * s : 288 * s + 288] = init_recv[s, :, 0:288]
        for f in range(2):
            po[f, :, 288 * s : 288 * s + 288] = unpack(po_recv[s, f].astype(F32)).astype(BF16)

    forward.send_back()
    forward.finish()
    prefix = forward.out

    def mixing(bd, m_ref, md_ref, s1, s2, s3, mbar, q_bar, adj):
        blocks = backward.blocks

        @pl.loop(0, 2)
        def _(f):
            pt, pdt = [], []
            for j in range(TILES):
                both = prefix[f, 144 * j : 144 * j + 144, :].astype(F32)
                pt.append(both[:HD] + init[:, 128 * j : 128 * j + 128])
                pdt.append(both[HD:])
            for t, heads in WINDOWS:
                bd[t] = block_diagonal(pt, t, heads)
                bdd = block_diagonal(pdt, t, heads)
                qw, qdw = window(q, f, t), window(qd, f, t)
                window_out(m_ref, 0, t, dot(qw, bd[t]))
                window_out(md_ref, 0, t, dot(qdw, bd[t]) + dot(qw, bdd))
            for t, heads in WINDOWS:
                ones = same_head(t, heads)
                lanes = slice(128 * t, 128 * t + 256)
                m, md, p = m_ref[0, :, lanes], md_ref[0, :, lanes], po[f, :, lanes].astype(F32)
                window_out(s1, 0, t, dot((m * m).astype(BF16), ones))
                window_out(s2, 0, t, dot((m * md).astype(BF16), ones))
                window_out(s3, 0, t, dot((m * p).astype(BF16), ones))
            m, md, p = m_ref[0], md_ref[0], po[f].astype(F32)
            scale = lax.rsqrt(s1[0] * (1.0 / HD) + 1e-6)
            pulled = m * (scale * scale * scale) * (1.0 / HD)
            mbar[0] = (p * scale - pulled * s3[0]).astype(BF16)
            fl = m * scale
            tg = md * scale - pulled * s2[0]
            for s in range(nsp):
                out_send[s, 0, f] = pack(fl[:, 288 * s : 288 * s + 288]).astype(BF16)
                out_send[s, 1, f] = pack(tg[:, 288 * s : 288 * s + 288]).astype(BF16)
            pb = [None] * TILES
            for t, heads in WINDOWS:
                mw = window(mbar, 0, t)
                window_out(s1, 0, t, dot(mw, bd[t], ((1,), (1,))))
                compact_add(pb, t, heads, dot(window(q, f, t), mw, ((0,), (0,))))
            q_bar[f] = s1[0].astype(BF16)
            pb.append(jnp.zeros((blocks.shape[1] - TILES * HD, 128), F32))
            blocks[f] = jnp.concatenate(pb, 0).astype(BF16)

        backward.start()

        @pl.loop(1, nsp)
        def _(i):
            exchange(place, out_send, out_recv, out_s, out_r, i).start()

        out_recv[sp] = out_send[sp]

        @pl.loop(0, 2)
        def _(f):
            adj[f] = dot(q_bar[f], q_w[...], ((1,), (1,)))

        backward.group_sums()
        backward.send_back()
        backward.finish()
        sc = backward.out

        @pl.loop(0, 2)
        def _(f):
            rows = sc[f].astype(F32)
            tiles = [rows[HD * j : HD * j + HD] for j in range(TILES)]
            for s in range(nsp):
                wide = jnp.concatenate(tiles[2 * s : 2 * s + 3], 1)[:, 32 * s : 32 * s + 288]
                parts = [wide[:, :128], wide[:, 128:256]]
                parts.append(jnp.concatenate([wide[:, 256:], jnp.zeros((HD, 96), F32)], 1))
                parts.append(jnp.zeros((8, 128), F32))
                cot_send[s, f] = jnp.concatenate(parts, 0).astype(BF16)

        @pl.loop(1, nsp)
        def _(i):
            exchange(place, cot_send, cot_recv, cot_s, cot_r, i).start()

        cot_recv[sp] = cot_send[sp]

        @pl.loop(0, 2)
        def _(f):
            rows = sc[f].astype(F32)
            tiles = [rows[HD * j : HD * j + HD] for j in range(TILES)]
            for t, heads in WINDOWS:
                b = block_diagonal(tiles, t, heads)
                window_out(s1, 0, t, dot(window(v, f, t), b, ((1,), (1,))))
                window_out(s2, 0, t, dot(window(k, f, t), b))
            total = adj[f] + dot(s1[0].astype(BF16), k_w[...], ((1,), (1,)))
            total = total + dot(s2[0].astype(BF16), v_w[...], ((1,), (1,)))
            adj_out[f] = total.astype(BF16)

    wide = pltpu.VMEM((1, TOK, D), F32)
    pl.run_scoped(
        mixing,
        pltpu.VMEM((8, 256, 256), BF16),
        wide,
        wide,
        wide,
        wide,
        wide,
        pltpu.VMEM((1, TOK, D), BF16),
        pltpu.VMEM((2, TOK, D), BF16),
        pltpu.VMEM((2, TOK, D), F32),
    )

    @pl.loop(1, nsp)
    def _(i):
        s, _ = place.mate(i)
        arrived(out_recv.at[s], out_r.at[s])
        arrived(cot_recv.at[s], cot_r.at[s])

    @pl.loop(0, nsp)
    def _(s):
        for f in range(2):
            flow_out[f, s] = unpack(out_recv[s, 0, f].astype(F32)).astype(BF16)
            tangent_out[f, s] = unpack(out_recv[s, 1, f].astype(F32)).astype(BF16)
            rows = cot_recv[s, f].astype(F32)
            lanes = jnp.concatenate([rows[HD * i : HD * i + HD] for i in range(3)], 1)
            for j in range(4):
                cot_out[f, s, j] = lanes[:, HD * j : HD * j + HD]

    @pl.loop(1, nsp)
    def _(i):
        exchange(place, po_send, po_recv, po_s, po_r, i).wait_send()
        init_move(i).wait_send()
        exchange(place, out_send, out_recv, out_s, out_r, i).wait_send()
        exchange(place, cot_send, cot_recv, cot_s, cot_r, i).wait_send()

    forward.drain()
    backward.drain()


def padded_rows(shape, rows):
    peers = min(4, shape[0]) * shape[1]
    return -(-rows // (16 * peers)) * 16 * peers


def on_device(shape, video, conv_weight, embed_weight, q_weight, k_weight, v_weight, initial_state, probe_in, probe_out):
    ntm, nsp = shape
    peers = min(4, ntm) * nsp
    dma = pltpu.SemaphoreType.DMA
    heads = jax.ShapeDtypeStruct((2, nsp, TOK, D // 4), BF16)
    rows = pltpu.VMEM((2, TOK, D), BF16)
    square = pltpu.VMEM((D, D), BF16)
    packed = pltpu.VMEM((nsp, 2, PACK, 128), BF16)
    twice = pltpu.VMEM((nsp, 2, 2, PACK, 128), BF16)
    cots = pltpu.VMEM((nsp, 2, 224, 128), BF16)
    four = dma((nsp,))
    flow, tangent, adjoint, cot = pl.pallas_call(
        functools.partial(kernel, shape),
        out_shape=[
            heads,
            heads,
            jax.ShapeDtypeStruct((2, TOK, D), BF16),
            jax.ShapeDtypeStruct((2, nsp, 4, HD, HD), F32),
        ],
        in_specs=[anywhere()] * 6 + [vmem()] + [anywhere()] * 2,
        out_specs=[vmem()] * 4,
        scratch_shapes=[
            pltpu.VMEM((4, TOK + 64, C), BF16),
            square,
            square,
            square,
            rows,
            rows,
            rows,
            rows,
            pltpu.VMEM((2 * TOK, D), BF16),
            packed,
            packed,
            rows,
            pltpu.VMEM((HD, 384), F32),
            pltpu.VMEM((nsp, HD, 384), F32),
            pltpu.VMEM((HD, D), F32),
            twice,
            twice,
            cots,
            cots,
            dma((5,)),
            dma((5,)),
            dma((7,)),
            dma,
            four,
            four,
            four,
            four,
            four,
            four,
            four,
            four,
        ]
        + scan_scratch(shape, padded_rows(shape, TILES * 2 * HD) // peers)
        + scan_scratch(shape, padded_rows(shape, TILES * HD) // peers),
        compiler_params=pltpu.CompilerParams(
            collective_id=0, has_side_effects=True, vmem_limit_bytes=VMEM_LIMIT
        ),
        name="flow_layer",
    )(
        video.reshape(2, TOK, C),
        conv_weight.reshape(9, 3 * C, C),
        embed_weight,
        q_weight,
        k_weight,
        v_weight,
        initial_state,
        probe_in.reshape(2 * TOK, D),
        probe_out.reshape(2, 4 * TOK, D // 4),
    )
    full = (2, 32, 32, D // 4)
    return (
        flow.reshape(full),
        tangent.reshape(full),
        adjoint.reshape(2, 8, 32, D),
        cot.reshape(8, 4, HD, HD),
    )


def solution(mesh):
    by_rows = P("tm", "space", None, None)
    by_heads = P("tm", None, None, "space")
    return jax.shard_map(
        functools.partial(on_device, (mesh.shape["tm"], mesh.shape["space"])),
        mesh=mesh,
        in_specs=(by_rows, P(), P(), P(), P(), P(), P("space", None, None), by_rows, by_heads),
        out_specs=(by_heads, by_heads, by_rows, by_rows),
        check_vma=False,
    )
```

profile of v0, /device:TPU:1, one launch (start us, length us, event | category | flops | bytes accessed | tf_op | source)
XLA Modules:
  0.0 131.2 jit_solution(5576364024446907577)
XLA Ops:
  0.6 123.2 %flow_layer.1 = (bf16[2,4,256,288]{3,2,1,0:T(8,128)(2,1)}, bf16[2,4,256,288]{3,2,1,0:T(8,128)(2,1)}, bf16[2,256,1152]{2,1,0:T(8,128)(2,1)}, f32[2,4,4,72,72]{4,3,2,1,0:T(8,128)}) custom-call(bf16[2,256,384]{2,1,0:T(8,128)(2,1)} %bitcast.15, bf16[9,1152,384]{2,1,0:T(8,128)(2,1)} %bitcast.8, bf16[384,1152]{1,0:T(8,128)(2,1)} %embed_h.1, ...), custom_call_target="tpu_custom_call" | custom-call | tf_op jit(solution)/shard_map/flow_layer/pallas_call | solution.py:654
  123.8 0.0 copy-start
  123.8 2.8 %copy.17 = bf16[2,32,32,288]{3,2,1,0:T(8,128)(2,1)} copy(bf16[2,32,32,288]{3,2,1,0:T(8,128)(2,1)} %bitcast.12) | data formatting | bytes 2359296
  126.6 0.0 copy-done
  126.6 0.0 copy-start.2
  126.6 1.1 copy.18
  127.8 0.7 copy-done.2
  128.5 0.0 copy-start.1
  128.5 1.0 copy.19
  129.5 0.7 copy-done.1
  130.2 1.0 copy.20
Async XLA Ops:
  123.8 2.8 %copy-start = (bf16[2,4,256,288]{3,2,1,0:T(8,128)(2,1)S(1)}, bf16[2,4,256,288]{3,2,1,0:T(8,128)(2,1)}, u32[]{:S(2)}) copy-start(bf16[2,4,256,288]{3,2,1,0:T(8,128)(2,1)} %get-tuple-element.9) | copy-start | bytes 3538948
  126.6 1.8 %copy-start.2 = (bf16[2,256,1152]{2,1,0:T(8,128)(2,1)S(1)}, bf16[2,256,1152]{2,1,0:T(8,128)(2,1)}, u32[]{:S(2)}) copy-start(bf16[2,256,1152]{2,1,0:T(8,128)(2,1)} %get-tuple-element.10) | copy-start | bytes 3538948
  128.5 1.7 %copy-start.1 = (f32[2,4,4,72,72]{4,3,2,1,0:T(8,128)S(1)}, f32[2,4,4,72,72]{4,3,2,1,0:T(8,128)}, u32[]{:S(2)}) copy-start(f32[2,4,4,72,72]{4,3,2,1,0:T(8,128)} %get-tuple-element.11) | copy-start | bytes 1990660
where the time goes:
time: 131 us
  Pallas kernels  123 us (94%)
  local copies, waits for them, and re-layouts  7.38 us (6%)
    pallas_call x1, Pallas kernels, on_device(): pl.pallas_call(functools.partial(kernel, shape), out_shape=[heads, heads,...  123 us
    unnamed x10, local copies, waits for them, and re-layouts  7.38 us

commit v1 on v0

v1 whole, which is shorter than its diff:
```python
import functools

import jax
import jax.numpy as jnp
from jax import lax
from jax.experimental import pallas as pl
from jax.experimental.pallas import tpu as pltpu
from jax.sharding import PartitionSpec as P

MESH = pl.DeviceIdType.MESH
F32 = jnp.float32
BF16 = jnp.bfloat16
D = 1152
HEADS = 16
HD = 72
C = 384
TOK = 256
TILES = D // 128
WINDOWS = (
    (0, (0, 1, 2)),
    (1, (3, 4)),
    (2, (5, 6)),
    (3, (7,)),
    (4, (8, 9)),
    (5, (10, 11)),
    (6, (12, 13)),
    (7, (14, 15)),
)
VMEM_LIMIT = 60 * 1024 * 1024


PARTS = ((WINDOWS[:4], 0, 5, (0, 1)), (WINDOWS[4:], 4, 5, (2, 3)))
COT = 176
PACK = 2 * TOK + TOK // 4


def vmem():
    return pl.BlockSpec(memory_space=pltpu.VMEM)


def anywhere():
    return pl.BlockSpec(memory_space=pl.ANY)


def dot(a, b, dims=((1,), (0,))):
    return lax.dot_general(a, b, (dims, ((), ())), preferred_element_type=F32)


def head_mask(h, tile, rows):
    lane = lax.broadcasted_iota(jnp.int32, (rows, 128), 1) + 128 * tile
    return (lane >= HD * h) & (lane < HD * (h + 1))


def compact_add(tiles, t, heads, g):
    for half in range(2):
        j = t + half
        for h in heads:
            if HD * h < 128 * (j + 1) and HD * (h + 1) > 128 * j:
                r = HD * h - 128 * t
                piece = g[r : r + HD, 128 * half : 128 * half + 128]
                piece = jnp.where(head_mask(h, j, HD), piece, 0.0)
                tiles[j] = tiles[j] + piece if j in tiles else piece


def block_diagonal(tiles, t, heads):
    halves = []
    for half in range(2):
        j = t + half
        parts = []
        at = 0
        for h in heads:
            r = HD * h - 128 * t
            if r > at:
                parts.append(jnp.zeros((r - at, 128), F32))
            if HD * h < 128 * (j + 1) and HD * (h + 1) > 128 * j:
                parts.append(jnp.where(head_mask(h, j, HD), tiles[j], 0.0))
            else:
                parts.append(jnp.zeros((HD, 128), F32))
            at = r + HD
        if at < 256:
            parts.append(jnp.zeros((256 - at, 128), F32))
        halves.append(jnp.concatenate(parts, 0))
    return jnp.concatenate(halves, 1).astype(BF16)


def same_head(t, heads):
    row = lax.broadcasted_iota(jnp.int32, (256, 256), 0) + 128 * t
    col = lax.broadcasted_iota(jnp.int32, (256, 256), 1) + 128 * t
    ok = None
    for h in heads:
        low, high = HD * h, HD * (h + 1)
        both = (row >= low) & (row < high) & (col >= low) & (col < high)
        ok = both if ok is None else ok | both
    return jnp.where(ok, 1.0, 0.0).astype(BF16)


def window_out(ref, t, value):
    if t == 0:
        ref[:, 0:256] = value
    else:
        ref[:, 128 * t : 128 * t + 128] = ref[:, 128 * t : 128 * t + 128] + value[:, :128]
        ref[:, 128 * t + 128 : 128 * t + 256] = value[:, 128:]


def pack(x):
    rest = x[:, 256:]
    rest = jnp.concatenate([rest[64 * i : 64 * i + 64] for i in range(4)], 1)
    return jnp.concatenate([x[:, :128], x[:, 128:256], rest], 0)


def unpack(x):
    rest = jnp.concatenate([x[2 * TOK :, 32 * i : 32 * i + 32] for i in range(4)], 0)
    return jnp.concatenate([x[:TOK], x[TOK : 2 * TOK], rest], 1)


def arrived(ref, sem):
    pltpu.make_async_copy(ref, ref, sem).wait()


def window(ref, f, t):
    return ref[f, :, 128 * t : 128 * t + 256]


class Place:
    def __init__(self, ntm, nsp):
        self.ntm, self.nsp = ntm, nsp
        self.nz, self.ny = min(4, ntm), nsp // 2
        self.tm, self.sp = lax.axis_index("tm"), lax.axis_index("space")
        self.peers, self.groups = self.nz * self.ny, ntm // self.nz
        self.group, self.z = self.tm // self.nz, self.tm % self.nz
        self.y, self.core = self.sp // 2, self.sp % 2
        self.me = self.z * self.ny + self.y
        self.twin = (self.tm, self.sp + 1 - 2 * self.core)

    def peer(self, k):
        p = lax.rem(self.me + k, self.peers)
        return p, (self.group * self.nz + p // self.ny, 2 * (p % self.ny) + self.core)

    def other(self, k):
        g = lax.rem(self.group + k, self.groups)
        return g, (g * self.nz + self.z, self.sp)

    def mate(self, k):
        s = lax.rem(self.sp + k, self.nsp)
        return s, (self.tm, s)


def remote(src, dst, send_sem, recv_sem, device):
    return pltpu.make_async_remote_copy(
        src_ref=src,
        dst_ref=dst,
        send_sem=send_sem,
        recv_sem=recv_sem,
        device_id=device,
        device_id_type=MESH,
    )


class Scan:
    def __init__(self, place, reverse, rows, blocks, out, pair, chip, got, sums, answer, back, theirs, totals, total,
                 s0, r0, s1, r1, s2, r2, s3, r3, s4, r4):
        self.place, self.reverse, self.rows = place, reverse, rows
        self.blocks, self.out, self.pair, self.chip, self.got = blocks, out, pair, chip, got
        self.sums, self.answer, self.back, self.theirs = sums, answer, back, theirs
        self.totals, self.total = totals, total
        self.s0, self.r0, self.s1, self.r1, self.s2, self.r2 = s0, r0, s1, r1, s2, r2
        self.s3, self.r3, self.s4, self.r4 = s3, r3, s4, r4
        self.share = got.shape[2]

    def half(self, c):
        n = self.chip.shape[1]
        return pl.ds(pl.multiple_of(c * n, n), n)

    def part(self, p):
        return pl.ds(pl.multiple_of(p * self.share, self.share), self.share)

    def used(self, p):
        return (self.place.core * self.place.peers + p) * self.share < self.rows

    def swap(self):
        return remote(
            self.blocks.at[:, self.half(1 - self.place.core)], self.pair, self.s0, self.r0, self.place.twin
        )

    def first(self, k):
        p, device = self.place.peer(k)
        me = self.place.me
        return remote(self.chip.at[:, self.part(p)], self.got.at[me], self.s1.at[p], self.r1.at[me], device)

    def second(self, k):
        g, device = self.place.other(k)
        mine = self.place.group
        return remote(self.total, self.totals.at[mine], self.s2.at[g], self.r2.at[mine], device)

    def third(self, k):
        p, device = self.place.peer(k)
        me = self.place.me
        return remote(self.answer.at[p], self.back.at[:, self.part(me)], self.s3.at[p], self.r3.at[me], device)

    def fourth(self):
        return remote(self.theirs, self.out.at[:, self.half(self.place.core)], self.s4, self.r4, self.place.twin)

    def start(self):
        self.swap().start()

    def spread(self):
        arrived(self.pair, self.r0)
        own = self.blocks[:, self.half(self.place.core)].astype(F32)
        self.chip[...] = (own + self.pair[...].astype(F32)).astype(BF16)

        @pl.loop(1, self.place.peers)
        def _(k):
            @pl.when(self.used(self.place.peer(k)[0]))
            def _():
                self.first(k).start()

    def group_sums(self):
        @pl.when(self.used(self.place.me))
        def _():
            self.got[self.place.me] = self.chip[:, self.part(self.place.me)]

            @pl.loop(1, self.place.peers)
            def _(k):
                p, _ = self.place.peer(k)
                arrived(self.got.at[p], self.r1.at[p])

            ny = self.place.ny
            running = jnp.zeros((self.share, 128), F32)
            order = [(zz * ny + y, f) for zz in range(self.place.nz) for f in range(2) for y in range(ny)]
            for p, f in reversed(order) if self.reverse else order:
                self.sums[p, f] = running
                running = running + self.got[p, f].astype(F32)
            self.total[...] = running.astype(BF16)

            @pl.loop(1, self.place.groups)
            def _(k):
                self.second(k).start()

            self.totals[self.place.group] = jnp.zeros((self.share, 128), BF16)

    def send_back(self):
        @pl.when(self.used(self.place.me))
        def _():
            @pl.loop(1, self.place.groups)
            def _(k):
                g, _ = self.place.other(k)
                arrived(self.totals.at[g], self.r2.at[g])

            group = self.place.group
            before = jnp.zeros((self.share, 128), F32)
            for g in range(self.place.groups):
                counts = g > group if self.reverse else g < group
                before = before + jnp.where(counts, self.totals[g].astype(F32), 0.0)
            for p in range(self.place.peers):
                self.answer[p] = (self.sums[p] + before[None]).astype(BF16)

            @pl.loop(1, self.place.peers)
            def _(k):
                self.third(k).start()

            self.back[:, self.part(self.place.me)] = self.answer[self.place.me]

    def pair_back(self):
        @pl.loop(1, self.place.peers)
        def _(k):
            p, _ = self.place.peer(k)

            @pl.when(self.used(p))
            def _():
                arrived(self.answer.at[p], self.r3.at[p])

        core = self.place.core
        here = self.half(core)
        before = self.back[...].astype(F32)
        own, pair = self.blocks[:, here].astype(F32), self.pair[...].astype(F32)
        after = core == (0 if self.reverse else 1)
        self.theirs[...] = (before + pair + jnp.where(after, 0.0, own)).astype(BF16)
        self.fourth().start()
        self.out[:, here] = (before + own + jnp.where(after, pair, 0.0)).astype(BF16)

    def finish(self):
        arrived(self.theirs, self.r4)

    def drain(self):
        self.swap().wait_send()
        self.fourth().wait_send()

        @pl.loop(1, self.place.peers)
        def _(k):
            @pl.when(self.used(self.place.peer(k)[0]))
            def _():
                self.first(k).wait_send()

        @pl.when(self.used(self.place.me))
        def _():
            @pl.loop(1, self.place.peers)
            def _(k):
                self.third(k).wait_send()

            @pl.loop(1, self.place.groups)
            def _(k):
                self.second(k).wait_send()


def scan_share(shape, rows):
    return -(-rows // (16 * 2 * min(4, shape[0]) * (shape[1] // 2))) * 16


def scan_scratch(shape, rows):
    ntm, nsp = shape
    nz = min(4, ntm)
    peers, groups = nz * (nsp // 2), ntm // nz
    share = scan_share(shape, rows)
    dma = pltpu.SemaphoreType.DMA
    full, half = pltpu.VMEM((2, 2 * peers * share, 128), BF16), pltpu.VMEM((2, peers * share, 128), BF16)
    shares = pltpu.VMEM((peers, 2, share, 128), BF16)
    return [
        full,
        full,
        half,
        half,
        shares,
        pltpu.VMEM((peers, 2, share, 128), F32),
        shares,
        half,
        half,
        pltpu.VMEM((groups, share, 128), BF16),
        pltpu.VMEM((share, 128), BF16),
        dma,
        dma,
        dma((peers,)),
        dma((peers,)),
        dma((groups,)),
        dma((groups,)),
        dma((peers,)),
        dma((peers,)),
        dma,
        dma,
    ]


def to_mate(place, send, recv, send_sem, recv_sem, s):
    me = place.sp
    return remote(send.at[s], recv.at[me], send_sem.at[s], recv_sem.at[me], (place.tm, s))


def give(place, send, recv, send_sem, recv_sem, targets):
    for s in targets:

        @pl.when(place.sp != s)
        def _():
            to_mate(place, send, recv, send_sem, recv_sem, s).start()

        @pl.when(place.sp == s)
        def _():
            recv[s] = send[s]


def kernel(
    shape,
    video, conv_h, embed_h, q_h, k_h, v_h, init_in, probe_h, po_h,
    flow_out, tangent_out, adj_out, cot_out,
    slab, q_w, k_w, v_w, q, qd, k, v, latent, po_send, po_recv, po, init_send, init_recv, init,
    out_send, out_recv, cot_send, cot_recv,
    halo_send, halo_recv, load, keep_sem, po_s, po_r, init_s, init_r, out_s, out_r, cot_s, cot_r,
    *scans,
):
    ntm, nsp = shape
    place = Place(ntm, nsp)
    tm, sp = place.tm, place.sp
    n = len(scans) // 4
    forward = [Scan(place, False, 5 * 2 * HD, *scans[i * n : i * n + n]) for i in range(2)]
    backward = [Scan(place, True, 5 * HD, *scans[i * n : i * n + n]) for i in range(2, 4)]

    later, earlier = tm + 1 < ntm, tm > 0
    down, up = sp + 1 < nsp, sp > 0
    last, first = pl.ds(TOK - 32, 32), pl.ds(0, 32)
    top, mid, bottom = pl.ds(0, 32), pl.ds(32, TOK), pl.ds(32 + TOK, 32)
    whole = pl.ds(0, TOK)
    prev, own = pl.ds(0, 2), pl.ds(2, 2)
    moves = (
        (down, up, last, own, top, (tm, sp + 1), (tm, sp - 1)),
        (up, down, first, own, bottom, (tm, sp - 1), (tm, sp + 1)),
        (later, earlier, whole, prev, mid, (tm + 1, sp), (tm - 1, sp)),
        (down & later, up & earlier, last, prev, top, (tm + 1, sp + 1), (tm - 1, sp - 1)),
        (up & later, down & earlier, first, prev, bottom, (tm + 1, sp - 1), (tm - 1, sp + 1)),
    )

    barrier = pltpu.get_barrier_semaphore()
    for _, may_recv, _, _, _, _, source in moves:

        @pl.when(may_recv)
        def _():
            pl.semaphore_signal(barrier, inc=1, device_id=source, device_id_type=MESH)

    def greet(count, device_of):
        @pl.loop(1, count)
        def _(i):
            pl.semaphore_signal(barrier, inc=1, device_id=device_of(i)[1], device_id_type=MESH)

    greet(place.groups, place.other)
    greet(place.peers, place.peer)
    greet(nsp, place.mate)

    def encode(conv_w, embed_w, probe, po_i, taps, acc, kd, vd):
        loads = [
            pltpu.make_async_copy(src, dst, load.at[i])
            for i, (src, dst) in enumerate(
                (
                    (po_h, po_i),
                    (probe_h, probe),
                    (k_h, k_w),
                    (v_h, v_w),
                    (conv_h, conv_w),
                    (q_h, q_w),
                    (embed_h, embed_w),
                )
            )
        ]
        keep = pltpu.make_async_copy(video, slab.at[own, mid], keep_sem)
        keep.start()
        for one in loads:
            one.start()

        for _, may_recv, _, frames, there, _, _ in moves:

            @pl.when(jnp.logical_not(may_recv))
            def _():
                slab[frames, there] = jnp.zeros((2, there.size, C), BF16)

        heads = [init_in[j] for j in range(4)]
        init_send[...] = jnp.concatenate(heads + [jnp.zeros((HD, 96), F32)], 1)
        for scan in forward:
            at = 5 * 2 * HD
            scan.blocks[:, at:, :] = jnp.zeros((2, scan.blocks.shape[1] - at, 128), BF16)

        greeted = place.groups + place.peers + nsp - 3
        pl.semaphore_wait(barrier, sum(m[0].astype(jnp.int32) for m in moves) + greeted)

        copies = []
        for i, (may_send, _, rows, frames, there, target, _) in enumerate(moves):
            copy = remote(video.at[:, rows], slab.at[frames, there], halo_send.at[i], halo_recv.at[i], target)
            copies.append(copy)

            @pl.when(may_send)
            def _():
                copy.start()

        loads[0].wait()
        for s in range(nsp):
            for f in range(2):
                po_send[s, f] = pack(po_i[f, TOK * s : TOK * s + TOK, :].astype(F32)).astype(BF16)
        give(place, po_send, po_recv, po_s, po_r, range(nsp))

        @pl.loop(1, nsp)
        def _(i):
            init_move(i).start()

        init_recv[sp] = init_send[...]

        col = lax.broadcasted_iota(jnp.int32, (TOK + 64, C), 0) % 32

        def build(f):
            here = slab[f].astype(F32)
            left = jnp.where(col == 0, 0.0, pltpu.roll(here, 1, 0))
            right = jnp.where(col == 31, 0.0, pltpu.roll(here, TOK + 63, 0))
            taps[f, :, 0:C] = left.astype(BF16)
            taps[f, :, C : 2 * C] = slab[f]
            taps[f, :, 2 * C : 3 * C] = right.astype(BF16)

        def halo_wait(i):
            @pl.when(moves[i][1])
            def _():
                copies[i].wait_recv()

        def convolve(a, out):
            @pl.loop(0, 3)
            def _(b):
                rows = pl.ds(pl.multiple_of(b * 32, 32), TOK)
                x = taps[a + out[0] : a + out[-1] + 1, rows, :].reshape(len(out) * TOK, 3 * C)
                here = slice(out[0] * TOK, (out[-1] + 1) * TOK)
                acc[here] += dot(x, conv_w[3 * a + b])

        acc[...] = jnp.zeros_like(acc)
        keep.wait()
        halo_wait(0)
        halo_wait(1)
        build(2)
        build(3)

        loads[1].wait()
        direction = probe[...].astype(F32).astype(BF16)
        for one, weight, out in zip(loads[2:4], (k_w, v_w), (kd, vd)):
            one.wait()
            out[...] = dot(direction, weight[...]).astype(BF16).reshape(2, TOK, D)

        loads[4].wait()
        convolve(2, (0, 1))
        convolve(1, (1,))
        loads[5].wait()
        qd[...] = dot(direction, q_w[...]).astype(BF16).reshape(2, TOK, D)
        halo_wait(2)
        halo_wait(3)
        halo_wait(4)
        build(0)
        build(1)
        convolve(1, (0,))
        convolve(0, (0, 1))

        u = acc[...]
        active = (u / (1.0 + jnp.exp(-u))).astype(BF16)
        loads[6].wait()
        latent[...] = dot(active, embed_w[...]).astype(BF16)
        for weight, out in zip((k_w, v_w), (k, v)):
            out[...] = dot(latent[...], weight[...]).astype(BF16).reshape(2, TOK, D)

        for scan, (windows, base, tiles, _) in zip(forward, PARTS):

            @pl.loop(0, 2)
            def _(f):
                st, sd = {}, {}
                over = ((0,), (0,))
                for t, heads in windows:
                    kw, vw = window(k, f, t), window(v, f, t)
                    compact_add(st, t, heads, dot(kw, vw, over))
                    both = dot(window(kd, f, t), vw, over) + dot(kw, window(vd, f, t), over)
                    compact_add(sd, t, heads, both)
                for j in range(tiles):
                    both = jnp.concatenate([st[base + j], sd[base + j]], 0)
                    scan.blocks[f, 144 * j : 144 * j + 144, :] = both.astype(BF16)

            scan.start()

        forward[0].spread()
        q[...] = dot(latent[...], q_w[...]).astype(BF16).reshape(2, TOK, D)
        for copy, (may_send, *_) in zip(copies, moves):

            @pl.when(may_send)
            def _():
                copy.wait_send()

    def init_move(i):
        _, device = place.mate(i)
        return remote(init_send, init_recv.at[sp], init_s.at[i], init_r.at[sp], device)

    pl.run_scoped(
        encode,
        pltpu.VMEM((9, 3 * C, C), BF16),
        pltpu.VMEM((C, D), BF16),
        pltpu.VMEM((2 * TOK, D), jnp.int32),
        pltpu.VMEM((2, 4 * TOK, D // 4), jnp.int32),
        pltpu.VMEM((4, TOK + 64, 3 * C), BF16),
        pltpu.VMEM((2 * TOK, C), F32),
        pltpu.VMEM((2, TOK, D), BF16),
        pltpu.VMEM((2, TOK, D), BF16),
    )

    forward[1].spread()
    forward[0].group_sums()
    forward[1].group_sums()

    @pl.loop(1, nsp)
    def _(i):
        s, _ = place.mate(i)
        arrived(po_recv.at[s], po_r.at[s])
        arrived(init_recv.at[s], init_r.at[s])

    for s in range(nsp):
        init[:, 288 * s : 288 * s + 288] = init_recv[s, :, 0:288]
        for f in range(2):
            po[f, :, 288 * s : 288 * s + 288] = unpack(po_recv[s, f].astype(F32)).astype(BF16)

    forward[0].send_back()
    forward[1].send_back()
    forward[0].pair_back()

    def mixing(bd, m_ref, md_ref, s1, s2, s3, mbar, q_bar, adj):
        def mix(i):
            windows, base, tiles, targets = PARTS[i]
            prefix, blocks = forward[i].out, backward[i].blocks
            part = slice(128 * base, 128 * (base + tiles))

            @pl.loop(0, 2)
            def _(f):
                pt, pdt = {}, {}
                for j in range(base, base + tiles):
                    both = prefix[f, 144 * (j - base) : 144 * (j - base) + 144, :].astype(F32)
                    pt[j] = both[:HD] + init[:, 128 * j : 128 * j + 128]
                    pdt[j] = both[HD:]
                for w, (t, heads) in enumerate(windows):
                    bd[w] = block_diagonal(pt, t, heads)
                    bdd = block_diagonal(pdt, t, heads)
                    qw, qdw = window(q, f, t), window(qd, f, t)
                    window_out(m_ref, t - base, dot(qw, bd[w]))
                    window_out(md_ref, t - base, dot(qdw, bd[w]) + dot(qw, bdd))
                for t, heads in windows:
                    ones = same_head(t, heads)
                    lanes = slice(128 * (t - base), 128 * (t - base) + 256)
                    m, md, p = m_ref[:, lanes], md_ref[:, lanes], window(po, f, t).astype(F32)
                    window_out(s1, t - base, dot((m * m).astype(BF16), ones))
                    window_out(s2, t - base, dot((m * md).astype(BF16), ones))
                    window_out(s3, t - base, dot((m * p).astype(BF16), ones))
                m, md, p = m_ref[...], md_ref[...], po[f, :, part].astype(F32)
                scale = lax.rsqrt(s1[...] * (1.0 / HD) + 1e-6)
                pulled = m * (scale * scale * scale) * (1.0 / HD)
                mbar[...] = (p * scale - pulled * s3[...]).astype(BF16)
                fl = m * scale
                tg = md * scale - pulled * s2[...]
                for s in targets:
                    at = 288 * s - 128 * base
                    out_send[s, 0, f] = pack(fl[:, at : at + 288]).astype(BF16)
                    out_send[s, 1, f] = pack(tg[:, at : at + 288]).astype(BF16)
                pb = {}
                for w, (t, heads) in enumerate(windows):
                    mw = mbar[:, 128 * (t - base) : 128 * (t - base) + 256]
                    window_out(s1, t - base, dot(mw, bd[w], ((1,), (1,))))
                    compact_add(pb, t, heads, dot(window(q, f, t), mw, ((0,), (0,))))
                q_bar[i, f] = s1[...].astype(BF16)
                pb = [pb[j] for j in range(base, base + tiles)]
                pb.append(jnp.zeros((blocks.shape[1] - tiles * HD, 128), F32))
                blocks[f] = jnp.concatenate(pb, 0).astype(BF16)

            backward[i].start()

        def settle(i, last):
            windows, base, tiles, targets = PARTS[i]
            sc = backward[i].out
            part = slice(128 * base, 128 * (base + tiles))

            def tiles_of(f):
                rows = sc[f].astype(F32)
                return {base + j: rows[HD * j : HD * j + HD] for j in range(tiles)}

            @pl.loop(0, 2)
            def _(f):
                state = tiles_of(f)
                for s in targets:
                    wide = jnp.concatenate([state[2 * s + j] for j in range(3)], 1)[:, 32 * s : 32 * s + 288]
                    rest = [wide[24 * j : 24 * j + 24, 256:] for j in range(3)]
                    rest = jnp.concatenate(rest + [jnp.zeros((24, 32), F32)], 1)
                    parts = [wide[:, :128], wide[:, 128:256], rest, jnp.zeros((8, 128), F32)]
                    cot_send[s, f] = jnp.concatenate(parts, 0).astype(BF16)

            give(place, cot_send, cot_recv, cot_s, cot_r, targets)

            @pl.loop(0, 2)
            def _(f):
                state = tiles_of(f)
                for t, heads in windows:
                    b = block_diagonal(state, t, heads)
                    window_out(s1, t - base, dot(window(v, f, t), b, ((1,), (1,))))
                    window_out(s2, t - base, dot(window(k, f, t), b))
                total = adj[f] + dot(s1[...].astype(BF16), k_w[:, part], ((1,), (1,)))
                total = total + dot(s2[...].astype(BF16), v_w[:, part], ((1,), (1,)))
                if last:
                    adj_out[f] = total.astype(BF16)
                else:
                    adj[f] = total

        forward[0].finish()
        mix(0)
        forward[1].pair_back()
        backward[0].spread()
        give(place, out_send, out_recv, out_s, out_r, PARTS[0][3])
        forward[1].finish()
        mix(1)
        backward[0].group_sums()
        backward[1].spread()
        give(place, out_send, out_recv, out_s, out_r, PARTS[1][3])

        @pl.loop(0, 2)
        def _(f):
            total = None
            for i, (_, base, tiles, _) in enumerate(PARTS):
                part = slice(128 * base, 128 * (base + tiles))
                piece = dot(q_bar[i, f], q_w[:, part], ((1,), (1,)))
                total = piece if total is None else total + piece
            adj[f] = total

        backward[1].group_sums()
        backward[0].send_back()
        backward[1].send_back()
        backward[0].pair_back()
        backward[0].finish()
        backward[1].pair_back()
        settle(0, False)
        backward[1].finish()
        settle(1, True)

    wide = pltpu.VMEM((TOK, 640), F32)
    pl.run_scoped(
        mixing,
        pltpu.VMEM((4, 256, 256), BF16),
        wide,
        wide,
        wide,
        wide,
        wide,
        pltpu.VMEM((TOK, 640), BF16),
        pltpu.VMEM((2, 2, TOK, 640), BF16),
        pltpu.VMEM((2, TOK, D), F32),
    )

    @pl.loop(1, nsp)
    def _(i):
        s, _ = place.mate(i)
        arrived(out_recv.at[s], out_r.at[s])
        arrived(cot_recv.at[s], cot_r.at[s])

    @pl.loop(0, nsp)
    def _(s):
        for f in range(2):
            flow_out[f, s] = unpack(out_recv[s, 0, f].astype(F32)).astype(BF16)
            tangent_out[f, s] = unpack(out_recv[s, 1, f].astype(F32)).astype(BF16)
            rows = cot_recv[s, f].astype(F32)
            rest = rows[2 * HD : 2 * HD + 24]
            rest = jnp.concatenate([rest[:, 32 * j : 32 * j + 32] for j in range(3)], 0)
            lanes = jnp.concatenate([rows[:HD], rows[HD : 2 * HD], rest], 1)
            for j in range(4):
                cot_out[f, s, j] = lanes[:, HD * j : HD * j + HD]

    @pl.loop(1, nsp)
    def _(i):
        s, _ = place.mate(i)
        to_mate(place, po_send, po_recv, po_s, po_r, s).wait_send()
        init_move(i).wait_send()
        to_mate(place, out_send, out_recv, out_s, out_r, s).wait_send()
        to_mate(place, cot_send, cot_recv, cot_s, cot_r, s).wait_send()

    for scan in forward + backward:
        scan.drain()


def on_device(shape, video, conv_weight, embed_weight, q_weight, k_weight, v_weight, initial_state, probe_in, probe_out):
    ntm, nsp = shape
    dma = pltpu.SemaphoreType.DMA
    heads = jax.ShapeDtypeStruct((2, nsp, TOK, D // 4), BF16)
    rows = pltpu.VMEM((2, TOK, D), BF16)
    square = pltpu.VMEM((D, D), BF16)
    packed = pltpu.VMEM((nsp, 2, PACK, 128), BF16)
    twice = pltpu.VMEM((nsp, 2, 2, PACK, 128), BF16)
    cots = pltpu.VMEM((nsp, 2, COT, 128), BF16)
    four = dma((nsp,))
    flow, tangent, adjoint, cot = pl.pallas_call(
        functools.partial(kernel, shape),
        out_shape=[
            heads,
            heads,
            jax.ShapeDtypeStruct((2, TOK, D), BF16),
            jax.ShapeDtypeStruct((2, nsp, 4, HD, HD), F32),
        ],
        in_specs=[anywhere()] * 6 + [vmem()] + [anywhere()] * 2,
        out_specs=[vmem()] * 4,
        scratch_shapes=[
            pltpu.VMEM((4, TOK + 64, C), BF16),
            square,
            square,
            square,
            rows,
            rows,
            rows,
            rows,
            pltpu.VMEM((2 * TOK, D), BF16),
            packed,
            packed,
            rows,
            pltpu.VMEM((HD, 384), F32),
            pltpu.VMEM((nsp, HD, 384), F32),
            pltpu.VMEM((HD, D), F32),
            twice,
            twice,
            cots,
            cots,
            dma((5,)),
            dma((5,)),
            dma((7,)),
            dma,
            four,
            four,
            four,
            four,
            four,
            four,
            four,
            four,
        ]
        + scan_scratch(shape, 5 * 2 * HD) * 2
        + scan_scratch(shape, 5 * HD) * 2,
        compiler_params=pltpu.CompilerParams(
            collective_id=0, has_side_effects=True, vmem_limit_bytes=VMEM_LIMIT
        ),
        name="flow_layer",
    )(
        video.reshape(2, TOK, C),
        conv_weight.reshape(9, 3 * C, C),
        embed_weight,
        q_weight,
        k_weight,
        v_weight,
        initial_state,
        probe_in.reshape(2 * TOK, D),
        probe_out.reshape(2, 4 * TOK, D // 4),
    )
    full = (2, 32, 32, D // 4)
    return (
        flow.reshape(full),
        tangent.reshape(full),
        adjoint.reshape(2, 8, 32, D),
        cot.reshape(8, 4, HD, HD),
    )


def solution(mesh):
    by_rows = P("tm", "space", None, None)
    by_heads = P("tm", None, None, "space")
    return jax.shard_map(
        functools.partial(on_device, (mesh.shape["tm"], mesh.shape["space"])),
        mesh=mesh,
        in_specs=(by_rows, P(), P(), P(), P(), P(), P("space", None, None), by_rows, by_heads),
        out_specs=(by_heads, by_heads, by_rows, by_rows),
        check_vma=False,
    )
```

time: 131 us -> 124 us (0.947); the launches traced: 131 us -> 123 us
  Pallas kernels: 123 us -> 115 us
    pallas_call x1, Pallas kernels: 123 us -> 115 us  [on_device(): pl.pallas_call(functools.partial(kernel, shape), out_shape=[heads, heads,...]
where the time goes in v1:
time: 124 us; the launch traced here: 123 us
  Pallas kernels  115 us (93%)
  local copies, waits for them, and re-layouts  7.38 us (6%)
    pallas_call x1, Pallas kernels, on_device(): pl.pallas_call(functools.partial(kernel, shape), out_shape=[heads, heads,...  115 us
    unnamed x10, local copies, waits for them, and re-layouts  7.38 us

profile of v1, /device:TPU:1, one launch (start us, length us, event | category | flops | bytes accessed | tf_op | source)
XLA Modules:
  0.0 122.9 jit_solution(14318019126975476966)
XLA Ops:
  0.6 114.8 %flow_layer.1 = (bf16[2,4,256,288]{3,2,1,0:T(8,128)(2,1)}, bf16[2,4,256,288]{3,2,1,0:T(8,128)(2,1)}, bf16[2,256,1152]{2,1,0:T(8,128)(2,1)}, f32[2,4,4,72,72]{4,3,2,1,0:T(8,128)}) custom-call(bf16[2,256,384]{2,1,0:T(8,128)(2,1)} %bitcast.15, bf16[9,1152,384]{2,1,0:T(8,128)(2,1)} %bitcast.8, bf16[384,1152]{1,0:T(8,128)(2,1)} %embed_h.1, ...), custom_call_target="tpu_custom_call" | custom-call | tf_op jit(solution)/shard_map/flow_layer/pallas_call | solution.py:744
  115.5 0.0 copy-start
  115.5 2.8 %copy.17 = bf16[2,32,32,288]{3,2,1,0:T(8,128)(2,1)} copy(bf16[2,32,32,288]{3,2,1,0:T(8,128)(2,1)} %bitcast.12) | data formatting | bytes 2359296
  118.3 0.0 copy-done
  118.3 0.0 copy-start.2
  118.3 1.1 copy.18
  119.5 0.7 copy-done.2
  120.2 0.0 copy-start.1
  120.2 1.0 copy.19
  121.2 0.7 copy-done.1
  121.9 1.0 copy.20
Async XLA Ops:
  115.5 2.8 %copy-start = (bf16[2,4,256,288]{3,2,1,0:T(8,128)(2,1)S(1)}, bf16[2,4,256,288]{3,2,1,0:T(8,128)(2,1)}, u32[]{:S(2)}) copy-start(bf16[2,4,256,288]{3,2,1,0:T(8,128)(2,1)} %get-tuple-element.9) | copy-start | bytes 3538948
  118.3 1.8 %copy-start.2 = (bf16[2,256,1152]{2,1,0:T(8,128)(2,1)S(1)}, bf16[2,256,1152]{2,1,0:T(8,128)(2,1)}, u32[]{:S(2)}) copy-start(bf16[2,256,1152]{2,1,0:T(8,128)(2,1)} %get-tuple-element.10) | copy-start | bytes 3538948
  120.2 1.7 %copy-start.1 = (f32[2,4,4,72,72]{4,3,2,1,0:T(8,128)S(1)}, f32[2,4,4,72,72]{4,3,2,1,0:T(8,128)}, u32[]{:S(2)}) copy-start(f32[2,4,4,72,72]{4,3,2,1,0:T(8,128)} %get-tuple-element.11) | copy-start | bytes 1990660

commit v2 on v1

--- a/solution.py
+++ b/solution.py
@@ -356,13 +356,30 @@
             recv[s] = send[s]
 
 
+def piece(place, send, recv, send_sem, recv_sem, s, *at):
+    me = (place.sp, *at)
+    there = (s, *at)
+    return remote(send.at[there], recv.at[me], send_sem.at[there], recv_sem.at[me], (place.tm, s))
+
+
+def give_piece(place, send, recv, send_sem, recv_sem, s, *at):
+    @pl.when(place.sp != s)
+    def _():
+        piece(place, send, recv, send_sem, recv_sem, s, *at).start()
+
+    @pl.when(place.sp == s)
+    def _():
+        there = (s, *at)
+        pltpu.make_async_copy(send.at[there], recv.at[there], recv_sem.at[there]).start()
+
+
 def kernel(
     shape,
     video, conv_h, embed_h, q_h, k_h, v_h, init_in, probe_h, po_h,
-    flow_out, tangent_out, adj_out, cot_out,
+    out_recv, pre_recv, cot_recv, adj_out,
     slab, q_w, k_w, v_w, q, qd, k, v, latent, po_send, po_recv, po, init_send, init_recv, init,
-    out_send, out_recv, cot_send, cot_recv,
-    halo_send, halo_recv, load, keep_sem, po_s, po_r, init_s, init_r, out_s, out_r, cot_s, cot_r,
+    out_send, cot_send, adj_send,
+    halo_send, halo_recv, load, keep_sem, po_s, po_r, init_s, init_r, out_s, out_r, cot_s, cot_r, adj_s, pre_s, pre_r,
     *scans,
 ):
     ntm, nsp = shape
@@ -450,13 +467,6 @@
         for s in range(nsp):
             for f in range(2):
                 po_send[s, f] = pack(po_i[f, TOK * s : TOK * s + TOK, :].astype(F32)).astype(BF16)
-        give(place, po_send, po_recv, po_s, po_r, range(nsp))
-
-        @pl.loop(1, nsp)
-        def _(i):
-            init_move(i).start()
-
-        init_recv[sp] = init_send[...]
 
         col = lax.broadcasted_iota(jnp.int32, (TOK + 64, C), 0) % 32
 
@@ -502,6 +512,13 @@
         halo_wait(2)
         halo_wait(3)
         halo_wait(4)
+
+        @pl.loop(1, nsp)
+        def _(i):
+            init_move(i).start()
+
+        init_recv[sp] = init_send[...]
+        give(place, po_send, po_recv, po_s, po_r, range(nsp))
         build(0)
         build(1)
         convolve(1, (0,))
@@ -533,11 +550,41 @@
 
         forward[0].spread()
         q[...] = dot(latent[...], q_w[...]).astype(BF16).reshape(2, TOK, D)
+        packed(0, q)
         for copy, (may_send, *_) in zip(copies, moves):
 
             @pl.when(may_send)
             def _():
                 copy.wait_send()
+
+    def packed(x, rows):
+        @pl.loop(0, 2)
+        def _(f):
+            for s in range(nsp):
+                out_send[s, x, f] = pack(rows[f, :, 288 * s : 288 * s + 288].astype(F32)).astype(BF16)
+
+    def leave(x, f):
+        for s in range(nsp):
+            give_piece(place, out_send, out_recv, out_s, out_r, s, x, f)
+
+    def prefix_piece(s):
+        i = s // 2
+        at = 144 * (2 * s - PARTS[i][1])
+        return forward[i].out.at[:, at : at + 432]
+
+    def prefix_move(s):
+        return remote(prefix_piece(s), pre_recv.at[sp], pre_s.at[s], pre_r.at[sp], (tm, s))
+
+    def prefixes(i):
+        for s in PARTS[i][3]:
+
+            @pl.when(sp != s)
+            def _():
+                prefix_move(s).start()
+
+            @pl.when(sp == s)
+            def _():
+                pltpu.make_async_copy(prefix_piece(s), pre_recv.at[s], pre_r.at[s]).start()
 
     def init_move(i):
         _, device = place.mate(i)
@@ -558,6 +605,8 @@
     forward[1].spread()
     forward[0].group_sums()
     forward[1].group_sums()
+    packed(1, qd)
+    leave(1, 0)
 
     @pl.loop(1, nsp)
     def _(i):
@@ -572,9 +621,10 @@
 
     forward[0].send_back()
     forward[1].send_back()
+    leave(1, 1)
     forward[0].pair_back()
 
-    def mixing(bd, m_ref, md_ref, s1, s2, s3, mbar, q_bar, adj):
+    def mixing(bd, m_ref, s1, s2, s3, mbar, q_bar, adj):
         def mix(i):
             windows, base, tiles, targets = PARTS[i]
             prefix, blocks = forward[i].out, backward[i].blocks
@@ -582,34 +632,23 @@
 
             @pl.loop(0, 2)
             def _(f):
-                pt, pdt = {}, {}
+                pt = {}
                 for j in range(base, base + tiles):
                     both = prefix[f, 144 * (j - base) : 144 * (j - base) + 144, :].astype(F32)
                     pt[j] = both[:HD] + init[:, 128 * j : 128 * j + 128]
-                    pdt[j] = both[HD:]
                 for w, (t, heads) in enumerate(windows):
                     bd[w] = block_diagonal(pt, t, heads)
-                    bdd = block_diagonal(pdt, t, heads)
-                    qw, qdw = window(q, f, t), window(qd, f, t)
-                    window_out(m_ref, t - base, dot(qw, bd[w]))
-                    window_out(md_ref, t - base, dot(qdw, bd[w]) + dot(qw, bdd))
+                    window_out(m_ref, t - base, dot(window(q, f, t), bd[w]))
                 for t, heads in windows:
                     ones = same_head(t, heads)
                     lanes = slice(128 * (t - base), 128 * (t - base) + 256)
-                    m, md, p = m_ref[:, lanes], md_ref[:, lanes], window(po, f, t).astype(F32)
+                    m, p = m_ref[:, lanes], window(po, f, t).astype(F32)
                     window_out(s1, t - base, dot((m * m).astype(BF16), ones))
-                    window_out(s2, t - base, dot((m * md).astype(BF16), ones))
                     window_out(s3, t - base, dot((m * p).astype(BF16), ones))
-                m, md, p = m_ref[...], md_ref[...], po[f, :, part].astype(F32)
+                m, p = m_ref[...], po[f, :, part].astype(F32)
                 scale = lax.rsqrt(s1[...] * (1.0 / HD) + 1e-6)
                 pulled = m * (scale * scale * scale) * (1.0 / HD)
                 mbar[...] = (p * scale - pulled * s3[...]).astype(BF16)
-                fl = m * scale
-                tg = md * scale - pulled * s2[...]
-                for s in targets:
-                    at = 288 * s - 128 * base
-                    out_send[s, 0, f] = pack(fl[:, at : at + 288]).astype(BF16)
-                    out_send[s, 1, f] = pack(tg[:, at : at + 288]).astype(BF16)
                 pb = {}
                 for w, (t, heads) in enumerate(windows):
                     mw = mbar[:, 128 * (t - base) : 128 * (t - base) + 256]
@@ -641,7 +680,8 @@
                     parts = [wide[:, :128], wide[:, 128:256], rest, jnp.zeros((8, 128), F32)]
                     cot_send[s, f] = jnp.concatenate(parts, 0).astype(BF16)
 
-            give(place, cot_send, cot_recv, cot_s, cot_r, targets)
+            for s in targets:
+                give_piece(place, cot_send, cot_recv, cot_s, cot_r, s)
 
             @pl.loop(0, 2)
             def _(f):
@@ -653,33 +693,36 @@
                 total = adj[f] + dot(s1[...].astype(BF16), k_w[:, part], ((1,), (1,)))
                 total = total + dot(s2[...].astype(BF16), v_w[:, part], ((1,), (1,)))
                 if last:
-                    adj_out[f] = total.astype(BF16)
+                    adj_send[f] = total.astype(BF16)
+                    pltpu.make_async_copy(adj_send.at[f], adj_out.at[f], adj_s.at[f]).start()
                 else:
                     adj[f] = total
 
         forward[0].finish()
+        prefixes(0)
         mix(0)
         forward[1].pair_back()
         backward[0].spread()
-        give(place, out_send, out_recv, out_s, out_r, PARTS[0][3])
         forward[1].finish()
+        prefixes(1)
         mix(1)
         backward[0].group_sums()
         backward[1].spread()
-        give(place, out_send, out_recv, out_s, out_r, PARTS[1][3])
 
         @pl.loop(0, 2)
         def _(f):
             total = None
             for i, (_, base, tiles, _) in enumerate(PARTS):
                 part = slice(128 * base, 128 * (base + tiles))
-                piece = dot(q_bar[i, f], q_w[:, part], ((1,), (1,)))
-                total = piece if total is None else total + piece
+                share = dot(q_bar[i, f], q_w[:, part], ((1,), (1,)))
+                total = share if total is None else total + share
             adj[f] = total
 
         backward[1].group_sums()
+        leave(0, 0)
         backward[0].send_back()
         backward[1].send_back()
+        leave(0, 1)
         backward[0].pair_back()
         backward[0].finish()
         backward[1].pair_back()
@@ -695,62 +738,179 @@
         wide,
         wide,
         wide,
-        wide,
         pltpu.VMEM((TOK, 640), BF16),
         pltpu.VMEM((2, 2, TOK, 640), BF16),
         pltpu.VMEM((2, TOK, D), F32),
     )
 
-    @pl.loop(1, nsp)
-    def _(i):
-        s, _ = place.mate(i)
-        arrived(out_recv.at[s], out_r.at[s])
-        arrived(cot_recv.at[s], cot_r.at[s])
-
     @pl.loop(0, nsp)
     def _(s):
-        for f in range(2):
-            flow_out[f, s] = unpack(out_recv[s, 0, f].astype(F32)).astype(BF16)
-            tangent_out[f, s] = unpack(out_recv[s, 1, f].astype(F32)).astype(BF16)
-            rows = cot_recv[s, f].astype(F32)
-            rest = rows[2 * HD : 2 * HD + 24]
-            rest = jnp.concatenate([rest[:, 32 * j : 32 * j + 32] for j in range(3)], 0)
-            lanes = jnp.concatenate([rows[:HD], rows[HD : 2 * HD], rest], 1)
-            for j in range(4):
-                cot_out[f, s, j] = lanes[:, HD * j : HD * j + HD]
+        for x in range(2):
+            for f in range(2):
+                arrived(out_recv.at[s, x, f], out_r.at[s, x, f])
+        arrived(cot_recv.at[s], cot_r.at[s])
+        arrived(pre_recv.at[s], pre_r.at[s])
+
+    for s in range(nsp):
+
+        @pl.when(sp != s)
+        def _():
+            prefix_move(s).wait_send()
 
     @pl.loop(1, nsp)
     def _(i):
         s, _ = place.mate(i)
         to_mate(place, po_send, po_recv, po_s, po_r, s).wait_send()
         init_move(i).wait_send()
-        to_mate(place, out_send, out_recv, out_s, out_r, s).wait_send()
-        to_mate(place, cot_send, cot_recv, cot_s, cot_r, s).wait_send()
+        for x in range(2):
+            for f in range(2):
+                piece(place, out_send, out_recv, out_s, out_r, s, x, f).wait_send()
+        piece(place, cot_send, cot_recv, cot_s, cot_r, s).wait_send()
+
+    for f in range(2):
+        pltpu.make_async_copy(adj_send.at[f], adj_out.at[f], adj_s.at[f]).wait()
 
     for scan in forward + backward:
         scan.drain()
+
+
+OWN = ((0, (0, 1, 2)), (1, (3,)))
+
+
+def flow_kernel(nsp, out_h, pre_h, cot_h, adj_h, init_in, flow_h, tangent_h, cot_out_h, adj_out_h,
+                out, pre, cot, adj, flow, tangent, cots, m_ref, md_ref, s1, s2, sems, done, adj_s):
+    sp = lax.axis_index("space")
+
+    def loads(i):
+        s, f = i // 2, i % 2
+        return (
+            pltpu.make_async_copy(out_h.at[s, :, f], out.at[i], sems.at[0, i]),
+            pltpu.make_async_copy(pre_h.at[s, f], pre.at[i], sems.at[1, i]),
+            pltpu.make_async_copy(cot_h.at[s, f], cot.at[i], sems.at[2, i]),
+        )
+
+    def stores(i):
+        s, f = i // 2, i % 2
+        return (
+            pltpu.make_async_copy(flow.at[i], flow_h.at[f, s], done.at[0, i]),
+            pltpu.make_async_copy(tangent.at[i], tangent_h.at[f, s], done.at[1, i]),
+            pltpu.make_async_copy(cots.at[i], cot_out_h.at[f, s], done.at[2, i]),
+        )
+
+    for i in range(2 * nsp):
+        for one in loads(i):
+            one.start()
+    take = pltpu.make_async_copy(adj_h, adj, adj_s.at[0])
+    take.start()
+
+    heads = [init_in[j] for j in range(4)]
+    init = jnp.concatenate(heads + [jnp.zeros((HD, 96), F32)], 1)
+    row = lax.broadcasted_iota(jnp.int32, (384, 384), 0)
+    col = lax.broadcasted_iota(jnp.int32, (384, 384), 1)
+    shift = jnp.where(row == col + 32 * sp, 1.0, 0.0).astype(BF16)
+    ones = [same_head(t, group) for t, group in OWN]
+
+    def queries(x):
+        rest = x[2 * TOK :].astype(F32)
+        rest = jnp.concatenate([rest[:, 32 * j : 32 * j + 32] for j in range(4)], 0)
+        rest = jnp.concatenate([rest, jnp.zeros((TOK, 96), F32)], 1).astype(BF16)
+        return jnp.concatenate([x[:TOK], x[TOK : 2 * TOK], rest], 1)
+
+    @pl.loop(0, 2 * nsp)
+    def _(i):
+        for one in loads(i):
+            one.wait()
+        q, qd = queries(out[i, 0]), queries(out[i, 1])
+        tiles = jnp.concatenate([pre[i, 144 * j : 144 * j + 144, :] for j in range(3)], 1)
+        tiles = dot(tiles, shift)
+        state, state_dot = tiles[:HD] + init, tiles[HD:]
+        pt = {j: state[:, 128 * j : 128 * j + 128] for j in range(3)}
+        pdt = {j: state_dot[:, 128 * j : 128 * j + 128] for j in range(3)}
+        for t, group in OWN:
+            lanes = slice(128 * t, 128 * t + 256)
+            b, bd = block_diagonal(pt, t, group), block_diagonal(pdt, t, group)
+            window_out(m_ref, t, dot(q[:, lanes], b))
+            window_out(md_ref, t, dot(qd[:, lanes], b) + dot(q[:, lanes], bd))
+        for (t, _), one in zip(OWN, ones):
+            lanes = slice(128 * t, 128 * t + 256)
+            m, md = m_ref[:, lanes], md_ref[:, lanes]
+            window_out(s1, t, dot((m * m).astype(BF16), one))
+            window_out(s2, t, dot((m * md).astype(BF16), one))
+        m, md = m_ref[...], md_ref[...]
+        scale = lax.rsqrt(s1[...] * (1.0 / HD) + 1e-6)
+        flow[i] = (m * scale).astype(BF16)[:, :288]
+        pulled = m * (scale * scale * scale) * (1.0 / HD)
+        tangent[i] = (md * scale - pulled * s2[...]).astype(BF16)[:, :288]
+        rows = cot[i].astype(F32)
+        rest = rows[2 * HD : 2 * HD + 24]
+        rest = jnp.concatenate([rest[:, 32 * j : 32 * j + 32] for j in range(3)], 0)
+        lanes = jnp.concatenate([rows[:HD], rows[HD : 2 * HD], rest], 1)
+        for j in range(4):
+            cots[i, j] = lanes[:, HD * j : HD * j + HD]
+        for one in stores(i):
+            one.start()
+
+    take.wait()
+    put = pltpu.make_async_copy(adj, adj_out_h, adj_s.at[1])
+    put.start()
+    for i in range(2 * nsp):
+        for one in stores(i):
+            one.wait()
+    put.wait()
+
+
+def flows(nsp, out, pre, cot, adj, init):
+    heads = jax.ShapeDtypeStruct((2, nsp, TOK, D // 4), BF16)
+    n = 2 * nsp
+    wide = pltpu.VMEM((TOK, 384), F32)
+    return pl.pallas_call(
+        functools.partial(flow_kernel, nsp),
+        out_shape=[
+            heads,
+            heads,
+            jax.ShapeDtypeStruct((2, nsp, 4, HD, HD), F32),
+            jax.ShapeDtypeStruct(adj.shape, BF16),
+        ],
+        in_specs=[anywhere()] * 4 + [vmem()],
+        out_specs=[anywhere()] * 4,
+        scratch_shapes=[
+            pltpu.VMEM((n, 2, PACK, 128), BF16),
+            pltpu.VMEM((n, 432, 128), BF16),
+            pltpu.VMEM((n, COT, 128), BF16),
+            pltpu.VMEM(adj.shape, BF16),
+            pltpu.VMEM((n, TOK, D // 4), BF16),
+            pltpu.VMEM((n, TOK, D // 4), BF16),
+            pltpu.VMEM((n, 4, HD, HD), F32),
+            wide,
+            wide,
+            wide,
+            wide,
+            pltpu.SemaphoreType.DMA((3, n)),
+            pltpu.SemaphoreType.DMA((3, n)),
+            pltpu.SemaphoreType.DMA((2,)),
+        ],
+        compiler_params=pltpu.CompilerParams(vmem_limit_bytes=VMEM_LIMIT),
+        name="flow",
+    )(out, pre, cot, adj, init)
 
 
 def on_device(shape, video, conv_weight, embed_weight, q_weight, k_weight, v_weight, initial_state, probe_in, probe_out):
     ntm, nsp = shape
     dma = pltpu.SemaphoreType.DMA
-    heads = jax.ShapeDtypeStruct((2, nsp, TOK, D // 4), BF16)
     rows = pltpu.VMEM((2, TOK, D), BF16)
     square = pltpu.VMEM((D, D), BF16)
     packed = pltpu.VMEM((nsp, 2, PACK, 128), BF16)
-    twice = pltpu.VMEM((nsp, 2, 2, PACK, 128), BF16)
-    cots = pltpu.VMEM((nsp, 2, COT, 128), BF16)
     four = dma((nsp,))
-    flow, tangent, adjoint, cot = pl.pallas_call(
+    out, pre, cot, adjoint = pl.pallas_call(
         functools.partial(kernel, shape),
         out_shape=[
-            heads,
-            heads,
+            jax.ShapeDtypeStruct((nsp, 2, 2, PACK, 128), BF16),
+            jax.ShapeDtypeStruct((nsp, 2, 432, 128), BF16),
+            jax.ShapeDtypeStruct((nsp, 2, COT, 128), BF16),
             jax.ShapeDtypeStruct((2, TOK, D), BF16),
-            jax.ShapeDtypeStruct((2, nsp, 4, HD, HD), F32),
         ],
         in_specs=[anywhere()] * 6 + [vmem()] + [anywhere()] * 2,
-        out_specs=[vmem()] * 4,
+        out_specs=[anywhere()] * 4,
         scratch_shapes=[
             pltpu.VMEM((4, TOK + 64, C), BF16),
             square,
@@ -767,10 +927,9 @@
             pltpu.VMEM((HD, 384), F32),
             pltpu.VMEM((nsp, HD, 384), F32),
             pltpu.VMEM((HD, D), F32),
-            twice,
-            twice,
-            cots,
-            cots,
+            pltpu.VMEM((nsp, 2, 2, PACK, 128), BF16),
+            pltpu.VMEM((nsp, 2, COT, 128), BF16),
+            rows,
             dma((5,)),
             dma((5,)),
             dma((7,)),
@@ -779,8 +938,11 @@
             four,
             four,
             four,
+            dma((nsp, 2, 2)),
+            dma((nsp, 2, 2)),
             four,
             four,
+            dma((2,)),
             four,
             four,
         ]
@@ -801,6 +963,7 @@
         probe_in.reshape(2 * TOK, D),
         probe_out.reshape(2, 4 * TOK, D // 4),
     )
+    flow, tangent, cot, adjoint = flows(nsp, out, pre, cot, adjoint, initial_state)
     full = (2, 32, 32, D // 4)
     return (
         flow.reshape(full),

time: 124 us -> 119 us (0.960)
  local copies, waits for them, and re-layouts: 7.38 us -> 0 us
    unnamed x10 -> x0, local copies, waits for them, and re-layouts: 7.38 us -> none
    pallas_call x1 -> x2, Pallas kernels: 115 us -> 116 us  [the longest x1 106 us: on_device(): pl.pallas_call(functools.partial(kernel, shape), out_shape=[jax.ShapeDtyp...]
where the time goes in v2:
time: 119 us; the launch traced here: 117 us
  Pallas kernels  116 us (97%)
    pallas_call x1, Pallas kernels, on_device(): pl.pallas_call(functools.partial(kernel, shape), out_shape=[jax.ShapeDtyp...  106 us
    pallas_call x1, Pallas kernels, flows(): pl.pallas_call(functools.partial(flow_kernel, nsp), out_shape=[heads, hea...  10.2 us

profile of v2, /device:TPU:1, one launch (start us, length us, event | category | flops | bytes accessed | tf_op | source)
XLA Modules:
  0.0 116.9 jit_solution(6523276629008573991)
XLA Ops:
  0.6 105.9 %flow_layer.1 = (bf16[4,2,2,576,128]{4,3,2,1,0:T(8,128)(2,1)}, bf16[4,2,432,128]{3,2,1,0:T(8,128)(2,1)}, bf16[4,2,176,128]{3,2,1,0:T(8,128)(2,1)}, bf16[2,256,1152]{2,1,0:T(8,128)(2,1)}) custom-call(bf16[2,256,384]{2,1,0:T(8,128)(2,1)} %bitcast.11, bf16[9,1152,384]{2,1,0:T(8,128)(2,1)} %bitcast.8, bf16[384,1152]{1,0:T(8,128)(2,1)} %embed_h.1, ...), custom_call_target="tpu_custom_call" | custom-call | tf_op jit(solution)/shard_map/flow_layer/pallas_call | solution.py:904
  106.5 10.2 %flow.1 = (bf16[2,4,256,288]{3,2,1,0:T(8,128)(2,1)}, bf16[2,4,256,288]{3,2,1,0:T(8,128)(2,1)}, f32[2,4,4,72,72]{4,3,2,1,0:T(8,128)}, bf16[2,256,1152]{2,1,0:T(8,128)(2,1)}) custom-call(bf16[4,2,2,576,128]{4,3,2,1,0:T(8,128)(2,1)} %get-tuple-element.12.out_h, bf16[4,2,432,128]{3,2,1,0:T(8,128)(2,1)} %get-tuple-element.13.pre_h, ...), custom_call_target="tpu_custom_call" | custom-call | tf_op jit(solution)/shard_map/flow/pallas_call | solution.py:866

commit v3 on v2

--- a/solution.py
+++ b/solution.py
@@ -376,10 +376,10 @@
 def kernel(
     shape,
     video, conv_h, embed_h, q_h, k_h, v_h, init_in, probe_h, po_h,
-    out_recv, pre_recv, cot_recv, adj_out,
+    out_recv, cot_recv, adj_out,
     slab, q_w, k_w, v_w, q, qd, k, v, latent, po_send, po_recv, po, init_send, init_recv, init,
     out_send, cot_send, adj_send,
-    halo_send, halo_recv, load, keep_sem, po_s, po_r, init_s, init_r, out_s, out_r, cot_s, cot_r, adj_s, pre_s, pre_r,
+    halo_send, halo_recv, load, keep_sem, po_s, po_r, init_s, init_r, out_s, out_r, cot_s, cot_r, adj_s,
     *scans,
 ):
     ntm, nsp = shape
@@ -550,41 +550,11 @@
 
         forward[0].spread()
         q[...] = dot(latent[...], q_w[...]).astype(BF16).reshape(2, TOK, D)
-        packed(0, q)
         for copy, (may_send, *_) in zip(copies, moves):
 
             @pl.when(may_send)
             def _():
                 copy.wait_send()
-
-    def packed(x, rows):
-        @pl.loop(0, 2)
-        def _(f):
-            for s in range(nsp):
-                out_send[s, x, f] = pack(rows[f, :, 288 * s : 288 * s + 288].astype(F32)).astype(BF16)
-
-    def leave(x, f):
-        for s in range(nsp):
-            give_piece(place, out_send, out_recv, out_s, out_r, s, x, f)
-
-    def prefix_piece(s):
-        i = s // 2
-        at = 144 * (2 * s - PARTS[i][1])
-        return forward[i].out.at[:, at : at + 432]
-
-    def prefix_move(s):
-        return remote(prefix_piece(s), pre_recv.at[sp], pre_s.at[s], pre_r.at[sp], (tm, s))
-
-    def prefixes(i):
-        for s in PARTS[i][3]:
-
-            @pl.when(sp != s)
-            def _():
-                prefix_move(s).start()
-
-            @pl.when(sp == s)
-            def _():
-                pltpu.make_async_copy(prefix_piece(s), pre_recv.at[s], pre_r.at[s]).start()
 
     def init_move(i):
         _, device = place.mate(i)
@@ -605,8 +575,6 @@
     forward[1].spread()
     forward[0].group_sums()
     forward[1].group_sums()
-    packed(1, qd)
-    leave(1, 0)
 
     @pl.loop(1, nsp)
     def _(i):
@@ -621,34 +589,59 @@
 
     forward[0].send_back()
     forward[1].send_back()
-    leave(1, 1)
     forward[0].pair_back()
 
-    def mixing(bd, m_ref, s1, s2, s3, mbar, q_bar, adj):
-        def mix(i):
+    def mixing(bd, m_ref, md_ref, s1, s2, s3, mbar, q_bar, adj):
+        def leave(x, f, across):
+            for s in range(nsp):
+                there = place.y != s // 2
+
+                @pl.when(there if across else jnp.logical_not(there))
+                def _():
+                    give_piece(place, out_send, out_recv, out_s, out_r, s, x, f)
+
+        def mix(i, early):
             windows, base, tiles, targets = PARTS[i]
             prefix, blocks = forward[i].out, backward[i].blocks
             part = slice(128 * base, 128 * (base + tiles))
 
             @pl.loop(0, 2)
             def _(f):
-                pt = {}
+                pt, pdt = {}, {}
                 for j in range(base, base + tiles):
                     both = prefix[f, 144 * (j - base) : 144 * (j - base) + 144, :].astype(F32)
                     pt[j] = both[:HD] + init[:, 128 * j : 128 * j + 128]
+                    pdt[j] = both[HD:]
                 for w, (t, heads) in enumerate(windows):
                     bd[w] = block_diagonal(pt, t, heads)
-                    window_out(m_ref, t - base, dot(window(q, f, t), bd[w]))
+                    bdd = block_diagonal(pdt, t, heads)
+                    qw, qdw = window(q, f, t), window(qd, f, t)
+                    window_out(m_ref, t - base, dot(qw, bd[w]))
+                    window_out(md_ref, t - base, dot(qdw, bd[w]) + dot(qw, bdd))
                 for t, heads in windows:
                     ones = same_head(t, heads)
                     lanes = slice(128 * (t - base), 128 * (t - base) + 256)
-                    m, p = m_ref[:, lanes], window(po, f, t).astype(F32)
+                    m, md, p = m_ref[:, lanes], md_ref[:, lanes], window(po, f, t).astype(F32)
                     window_out(s1, t - base, dot((m * m).astype(BF16), ones))
+                    window_out(s2, t - base, dot((m * md).astype(BF16), ones))
                     window_out(s3, t - base, dot((m * p).astype(BF16), ones))
-                m, p = m_ref[...], po[f, :, part].astype(F32)
+                m, md, p = m_ref[...], md_ref[...], po[f, :, part].astype(F32)
                 scale = lax.rsqrt(s1[...] * (1.0 / HD) + 1e-6)
                 pulled = m * (scale * scale * scale) * (1.0 / HD)
                 mbar[...] = (p * scale - pulled * s3[...]).astype(BF16)
+                fl = m * scale
+                tg = md * scale - pulled * s2[...]
+                for s in targets:
+                    at = 288 * s - 128 * base
+                    out_send[s, 0, f] = pack(fl[:, at : at + 288]).astype(BF16)
+                    out_send[s, 1, f] = pack(tg[:, at : at + 288]).astype(BF16)
+                if early:
+
+                    @pl.when(f == 0)
+                    def _():
+                        leave(0, 0, True)
+                        leave(1, 0, True)
+
                 pb = {}
                 for w, (t, heads) in enumerate(windows):
                     mw = mbar[:, 128 * (t - base) : 128 * (t - base) + 256]
@@ -699,15 +692,29 @@
                     adj[f] = total
 
         forward[0].finish()
-        prefixes(0)
-        mix(0)
+
+        @pl.when(place.y == 1)
+        def _():
+            mix(0, True)
+
         forward[1].pair_back()
+        forward[1].finish()
+
+        @pl.when(place.y == 0)
+        def _():
+            mix(1, True)
+            mix(0, False)
+
+        @pl.when(place.y == 1)
+        def _():
+            mix(1, False)
+
         backward[0].spread()
-        forward[1].finish()
-        prefixes(1)
-        mix(1)
-        backward[0].group_sums()
         backward[1].spread()
+        leave(0, 1, True)
+        for f in range(2):
+            leave(0, f, False)
+            leave(1, f, False)
 
         @pl.loop(0, 2)
         def _(f):
@@ -718,11 +725,11 @@
                 total = share if total is None else total + share
             adj[f] = total
 
+        backward[0].group_sums()
         backward[1].group_sums()
-        leave(0, 0)
         backward[0].send_back()
         backward[1].send_back()
-        leave(0, 1)
+        leave(1, 1, True)
         backward[0].pair_back()
         backward[0].finish()
         backward[1].pair_back()
@@ -738,6 +745,7 @@
         wide,
         wide,
         wide,
+        wide,
         pltpu.VMEM((TOK, 640), BF16),
         pltpu.VMEM((2, 2, TOK, 640), BF16),
         pltpu.VMEM((2, TOK, D), F32),
@@ -749,13 +757,6 @@
             for f in range(2):
                 arrived(out_recv.at[s, x, f], out_r.at[s, x, f])
         arrived(cot_recv.at[s], cot_r.at[s])
-        arrived(pre_recv.at[s], pre_r.at[s])
-
-    for s in range(nsp):
-
-        @pl.when(sp != s)
-        def _():
-            prefix_move(s).wait_send()
 
     @pl.loop(1, nsp)
     def _(i):
@@ -774,19 +775,13 @@
         scan.drain()
 
 
-OWN = ((0, (0, 1, 2)), (1, (3,)))
-
-
-def flow_kernel(nsp, out_h, pre_h, cot_h, adj_h, init_in, flow_h, tangent_h, cot_out_h, adj_out_h,
-                out, pre, cot, adj, flow, tangent, cots, m_ref, md_ref, s1, s2, sems, done, adj_s):
-    sp = lax.axis_index("space")
-
+def unpack_kernel(nsp, out_h, cot_h, adj_h, flow_h, tangent_h, cot_out_h, adj_out_h,
+                  out, cot, flow, tangent, cots, sems, done, adj_s):
     def loads(i):
         s, f = i // 2, i % 2
         return (
             pltpu.make_async_copy(out_h.at[s, :, f], out.at[i], sems.at[0, i]),
-            pltpu.make_async_copy(pre_h.at[s, f], pre.at[i], sems.at[1, i]),
-            pltpu.make_async_copy(cot_h.at[s, f], cot.at[i], sems.at[2, i]),
+            pltpu.make_async_copy(cot_h.at[s, f], cot.at[i], sems.at[1, i]),
         )
 
     def stores(i):
@@ -800,47 +795,19 @@
     for i in range(2 * nsp):
         for one in loads(i):
             one.start()
-    take = pltpu.make_async_copy(adj_h, adj, adj_s.at[0])
-    take.start()
-
-    heads = [init_in[j] for j in range(4)]
-    init = jnp.concatenate(heads + [jnp.zeros((HD, 96), F32)], 1)
-    row = lax.broadcasted_iota(jnp.int32, (384, 384), 0)
-    col = lax.broadcasted_iota(jnp.int32, (384, 384), 1)
-    shift = jnp.where(row == col + 32 * sp, 1.0, 0.0).astype(BF16)
-    ones = [same_head(t, group) for t, group in OWN]
-
-    def queries(x):
-        rest = x[2 * TOK :].astype(F32)
-        rest = jnp.concatenate([rest[:, 32 * j : 32 * j + 32] for j in range(4)], 0)
-        rest = jnp.concatenate([rest, jnp.zeros((TOK, 96), F32)], 1).astype(BF16)
-        return jnp.concatenate([x[:TOK], x[TOK : 2 * TOK], rest], 1)
+    through = pltpu.make_async_copy(adj_h, adj_out_h, adj_s)
+    through.start()
 
     @pl.loop(0, 2 * nsp)
     def _(i):
         for one in loads(i):
             one.wait()
-        q, qd = queries(out[i, 0]), queries(out[i, 1])
-        tiles = jnp.concatenate([pre[i, 144 * j : 144 * j + 144, :] for j in range(3)], 1)
-        tiles = dot(tiles, shift)
-        state, state_dot = tiles[:HD] + init, tiles[HD:]
-        pt = {j: state[:, 128 * j : 128 * j + 128] for j in range(3)}
-        pdt = {j: state_dot[:, 128 * j : 128 * j + 128] for j in range(3)}
-        for t, group in OWN:
-            lanes = slice(128 * t, 128 * t + 256)
-            b, bd = block_diagonal(pt, t, group), block_diagonal(pdt, t, group)
-            window_out(m_ref, t, dot(q[:, lanes], b))
-            window_out(md_ref, t, dot(qd[:, lanes], b) + dot(q[:, lanes], bd))
-        for (t, _), one in zip(OWN, ones):
-            lanes = slice(128 * t, 128 * t + 256)
-            m, md = m_ref[:, lanes], md_ref[:, lanes]
-            window_out(s1, t, dot((m * m).astype(BF16), one))
-            window_out(s2, t, dot((m * md).astype(BF16), one))
-        m, md = m_ref[...], md_ref[...]
-        scale = lax.rsqrt(s1[...] * (1.0 / HD) + 1e-6)
-        flow[i] = (m * scale).astype(BF16)[:, :288]
-        pulled = m * (scale * scale * scale) * (1.0 / HD)
-        tangent[i] = (md * scale - pulled * s2[...]).astype(BF16)[:, :288]
+        for x, to in enumerate((flow, tangent)):
+            to[i, :, 0:128] = out[i, x, 0:TOK]
+            to[i, :, 128:256] = out[i, x, TOK : 2 * TOK]
+            rest = out[i, x, 2 * TOK :]
+            for j in range(4):
+                to[i, 64 * j : 64 * j + 64, 256:288] = rest[:, 32 * j : 32 * j + 32]
         rows = cot[i].astype(F32)
         rest = rows[2 * HD : 2 * HD + 24]
         rest = jnp.concatenate([rest[:, 32 * j : 32 * j + 32] for j in range(3)], 0)
@@ -850,48 +817,38 @@
         for one in stores(i):
             one.start()
 
-    take.wait()
-    put = pltpu.make_async_copy(adj, adj_out_h, adj_s.at[1])
-    put.start()
     for i in range(2 * nsp):
         for one in stores(i):
             one.wait()
-    put.wait()
-
-
-def flows(nsp, out, pre, cot, adj, init):
+    through.wait()
+
+
+def unpacked(nsp, out, cot, adj):
     heads = jax.ShapeDtypeStruct((2, nsp, TOK, D // 4), BF16)
     n = 2 * nsp
-    wide = pltpu.VMEM((TOK, 384), F32)
     return pl.pallas_call(
-        functools.partial(flow_kernel, nsp),
+        functools.partial(unpack_kernel, nsp),
         out_shape=[
             heads,
             heads,
             jax.ShapeDtypeStruct((2, nsp, 4, HD, HD), F32),
             jax.ShapeDtypeStruct(adj.shape, BF16),
         ],
-        in_specs=[anywhere()] * 4 + [vmem()],
+        in_specs=[anywhere()] * 3,
         out_specs=[anywhere()] * 4,
         scratch_shapes=[
             pltpu.VMEM((n, 2, PACK, 128), BF16),
-            pltpu.VMEM((n, 432, 128), BF16),
             pltpu.VMEM((n, COT, 128), BF16),
-            pltpu.VMEM(adj.shape, BF16),
             pltpu.VMEM((n, TOK, D // 4), BF16),
             pltpu.VMEM((n, TOK, D // 4), BF16),
             pltpu.VMEM((n, 4, HD, HD), F32),
-            wide,
-            wide,
-            wide,
-            wide,
+            pltpu.SemaphoreType.DMA((2, n)),
             pltpu.SemaphoreType.DMA((3, n)),
-            pltpu.SemaphoreType.DMA((3, n)),
-            pltpu.SemaphoreType.DMA((2,)),
+            pltpu.SemaphoreType.DMA,
         ],
         compiler_params=pltpu.CompilerParams(vmem_limit_bytes=VMEM_LIMIT),
-        name="flow",
-    )(out, pre, cot, adj, init)
+        name="unpack",
+    )(out, cot, adj)
 
 
 def on_device(shape, video, conv_weight, embed_weight, q_weight, k_weight, v_weight, initial_state, probe_in, probe_out):
@@ -901,16 +858,15 @@
     square = pltpu.VMEM((D, D), BF16)
     packed = pltpu.VMEM((nsp, 2, PACK, 128), BF16)
     four = dma((nsp,))
-    out, pre, cot, adjoint = pl.pallas_call(
+    out, cot, adjoint = pl.pallas_call(
         functools.partial(kernel, shape),
         out_shape=[
             jax.ShapeDtypeStruct((nsp, 2, 2, PACK, 128), BF16),
-            jax.ShapeDtypeStruct((nsp, 2, 432, 128), BF16),
             jax.ShapeDtypeStruct((nsp, 2, COT, 128), BF16),
             jax.ShapeDtypeStruct((2, TOK, D), BF16),
         ],
         in_specs=[anywhere()] * 6 + [vmem()] + [anywhere()] * 2,
-        out_specs=[anywhere()] * 4,
+        out_specs=[anywhere()] * 3,
         scratch_shapes=[
             pltpu.VMEM((4, TOK + 64, C), BF16),
             square,
@@ -943,8 +899,6 @@
             four,
             four,
             dma((2,)),
-            four,
-            four,
         ]
         + scan_scratch(shape, 5 * 2 * HD) * 2
         + scan_scratch(shape, 5 * HD) * 2,
@@ -963,7 +917,7 @@
         probe_in.reshape(2 * TOK, D),
         probe_out.reshape(2, 4 * TOK, D // 4),
     )
-    flow, tangent, cot, adjoint = flows(nsp, out, pre, cot, adjoint, initial_state)
+    flow, tangent, cot, adjoint = unpacked(nsp, out, cot, adjoint)
     full = (2, 32, 32, D // 4)
     return (
         flow.reshape(full),

time: 119 us -> 140 us (1.18); the launches traced: 117 us -> 140 us
  Pallas kernels: 116 us -> 139 us
    pallas_call x1, Pallas kernels: 10.2 us -> 37.2 us  [unpacked(): pl.pallas_call(functools.partial(unpack_kernel, nsp), out_shape=[heads, h...]
    pallas_call x1, Pallas kernels: 106 us -> 102 us  [on_device(): pl.pallas_call(functools.partial(kernel, shape), out_shape=[jax.ShapeDtyp...]
where the time goes in v3:
time: 140 us
  Pallas kernels  139 us (99%)
    pallas_call x1, Pallas kernels, on_device(): pl.pallas_call(functools.partial(kernel, shape), out_shape=[jax.ShapeDtyp...  102 us
    pallas_call x1, Pallas kernels, unpacked(): pl.pallas_call(functools.partial(unpack_kernel, nsp), out_shape=[heads, h...  37.2 us

profile of v3, /device:TPU:1, one launch (start us, length us, event | category | flops | bytes accessed | tf_op | source)
XLA Modules:
  0.0 140.3 jit_solution(17108641814150083306)
XLA Ops:
  0.6 102.3 %flow_layer.1 = (bf16[4,2,2,576,128]{4,3,2,1,0:T(8,128)(2,1)}, bf16[4,2,176,128]{3,2,1,0:T(8,128)(2,1)}, bf16[2,256,1152]{2,1,0:T(8,128)(2,1)}) custom-call(bf16[2,256,384]{2,1,0:T(8,128)(2,1)} %bitcast.11, bf16[9,1152,384]{2,1,0:T(8,128)(2,1)} %bitcast.8, bf16[384,1152]{1,0:T(8,128)(2,1)} %embed_h.1, bf16[1152,1152]{1,0:T(8,128)(2,1)} %q_h.1, ...), custom_call_target="tpu_custom_call" | custom-call | tf_op jit(solution)/shard_map/flow_layer/pallas_call | solution.py:861
  102.9 37.2 %unpack.1 = (bf16[2,4,256,288]{3,2,1,0:T(8,128)(2,1)}, bf16[2,4,256,288]{3,2,1,0:T(8,128)(2,1)}, f32[2,4,4,72,72]{4,3,2,1,0:T(8,128)}, bf16[2,256,1152]{2,1,0:T(8,128)(2,1)}) custom-call(bf16[4,2,2,576,128]{4,3,2,1,0:T(8,128)(2,1)} %get-tuple-element.11.out_h, bf16[4,2,176,128]{3,2,1,0:T(8,128)(2,1)} %get-tuple-element.12.cot_h, ...), custom_call_target="tpu_custom_call" | custom-call | tf_op jit(solution)/shard_map/unpack/pallas_call | solution.py:829

commit v4 on v3

--- a/solution.py
+++ b/solution.py
@@ -776,7 +776,7 @@
 
 
 def unpack_kernel(nsp, out_h, cot_h, adj_h, flow_h, tangent_h, cot_out_h, adj_out_h,
-                  out, cot, flow, tangent, cots, sems, done, adj_s):
+                  out, cot, adj, flow, tangent, cots, sems, done, adj_s):
     def loads(i):
         s, f = i // 2, i % 2
         return (
@@ -792,11 +792,14 @@
             pltpu.make_async_copy(cots.at[i], cot_out_h.at[f, s], done.at[2, i]),
         )
 
+    take = pltpu.make_async_copy(adj_h, adj, adj_s.at[0])
+    put = pltpu.make_async_copy(adj, adj_out_h, adj_s.at[1])
+    take.start()
     for i in range(2 * nsp):
         for one in loads(i):
             one.start()
-    through = pltpu.make_async_copy(adj_h, adj_out_h, adj_s)
-    through.start()
+    take.wait()
+    put.start()
 
     @pl.loop(0, 2 * nsp)
     def _(i):
@@ -820,7 +823,7 @@
     for i in range(2 * nsp):
         for one in stores(i):
             one.wait()
-    through.wait()
+    put.wait()
 
 
 def unpacked(nsp, out, cot, adj):
@@ -839,12 +842,13 @@
         scratch_shapes=[
             pltpu.VMEM((n, 2, PACK, 128), BF16),
             pltpu.VMEM((n, COT, 128), BF16),
+            pltpu.VMEM(adj.shape, BF16),
             pltpu.VMEM((n, TOK, D // 4), BF16),
             pltpu.VMEM((n, TOK, D // 4), BF16),
             pltpu.VMEM((n, 4, HD, HD), F32),
             pltpu.SemaphoreType.DMA((2, n)),
             pltpu.SemaphoreType.DMA((3, n)),
-            pltpu.SemaphoreType.DMA,
+            pltpu.SemaphoreType.DMA((2,)),
         ],
         compiler_params=pltpu.CompilerParams(vmem_limit_bytes=VMEM_LIMIT),
         name="unpack",

time: 140 us -> 108 us (0.77)
  Pallas kernels: 139 us -> 107 us
    pallas_call x1, Pallas kernels: 37.2 us -> 4.87 us  [unpacked(): pl.pallas_call(functools.partial(unpack_kernel, nsp), out_shape=[heads, h...]
where the time goes in v4:
time: 108 us
  Pallas kernels  107 us (99%)
    pallas_call x1, Pallas kernels, on_device(): pl.pallas_call(functools.partial(kernel, shape), out_shape=[jax.ShapeDtyp...  102 us
    pallas_call x1, Pallas kernels, unpacked(): pl.pallas_call(functools.partial(unpack_kernel, nsp), out_shape=[heads, h...  4.87 us

profile of v4, /device:TPU:1, one launch (start us, length us, event | category | flops | bytes accessed | tf_op | source)
XLA Modules:
  0.0 108.0 jit_solution(13380958836015107360)
XLA Ops:
  0.6 102.3 %flow_layer.1 = (bf16[4,2,2,576,128]{4,3,2,1,0:T(8,128)(2,1)}, bf16[4,2,176,128]{3,2,1,0:T(8,128)(2,1)}, bf16[2,256,1152]{2,1,0:T(8,128)(2,1)}) custom-call(bf16[2,256,384]{2,1,0:T(8,128)(2,1)} %bitcast.11, bf16[9,1152,384]{2,1,0:T(8,128)(2,1)} %bitcast.8, bf16[384,1152]{1,0:T(8,128)(2,1)} %embed_h.1, bf16[1152,1152]{1,0:T(8,128)(2,1)} %q_h.1, ...), custom_call_target="tpu_custom_call" | custom-call | tf_op jit(solution)/shard_map/flow_layer/pallas_call | solution.py:865
  102.9 4.9 %unpack.1 = (bf16[2,4,256,288]{3,2,1,0:T(8,128)(2,1)}, bf16[2,4,256,288]{3,2,1,0:T(8,128)(2,1)}, f32[2,4,4,72,72]{4,3,2,1,0:T(8,128)}, bf16[2,256,1152]{2,1,0:T(8,128)(2,1)}) custom-call(bf16[4,2,2,576,128]{4,3,2,1,0:T(8,128)(2,1)} %get-tuple-element.11.out_h, bf16[4,2,176,128]{3,2,1,0:T(8,128)(2,1)} %get-tuple-element.12.cot_h, ...), custom_call_target="tpu_custom_call" | custom-call | tf_op jit(solution)/shard_map/unpack/pallas_call | solution.py:832

commit v5 on v4

--- a/solution.py
+++ b/solution.py
@@ -549,6 +549,7 @@
             scan.start()
 
         forward[0].spread()
+        forward[1].spread()
         q[...] = dot(latent[...], q_w[...]).astype(BF16).reshape(2, TOK, D)
         for copy, (may_send, *_) in zip(copies, moves):
 
@@ -572,7 +573,6 @@
         pltpu.VMEM((2, TOK, D), BF16),
     )
 
-    forward[1].spread()
     forward[0].group_sums()
     forward[1].group_sums()
 

time: 108 us -> 108 us (level)
  no operation moved by 1% of the time
where the time goes in v5:
time: 108 us
  Pallas kernels  107 us (99%)
    pallas_call x1, Pallas kernels, on_device(): pl.pallas_call(functools.partial(kernel, shape), out_shape=[jax.ShapeDtyp...  102 us
    pallas_call x1, Pallas kernels, unpacked(): pl.pallas_call(functools.partial(unpack_kernel, nsp), out_shape=[heads, h...  4.87 us

profile of v5, /device:TPU:1, one launch (start us, length us, event | category | flops | bytes accessed | tf_op | source)
XLA Modules:
  0.0 108.0 jit_solution(2075902565866292585)
XLA Ops:
  0.6 102.3 %flow_layer.1 = (bf16[4,2,2,576,128]{4,3,2,1,0:T(8,128)(2,1)}, bf16[4,2,176,128]{3,2,1,0:T(8,128)(2,1)}, bf16[2,256,1152]{2,1,0:T(8,128)(2,1)}) custom-call(bf16[2,256,384]{2,1,0:T(8,128)(2,1)} %bitcast.11, bf16[9,1152,384]{2,1,0:T(8,128)(2,1)} %bitcast.8, bf16[384,1152]{1,0:T(8,128)(2,1)} %embed_h.1, bf16[1152,1152]{1,0:T(8,128)(2,1)} %q_h.1, ...), custom_call_target="tpu_custom_call" | custom-call | tf_op jit(solution)/shard_map/flow_layer/pallas_call | solution.py:865
  102.9 4.9 %unpack.1 = (bf16[2,4,256,288]{3,2,1,0:T(8,128)(2,1)}, bf16[2,4,256,288]{3,2,1,0:T(8,128)(2,1)}, f32[2,4,4,72,72]{4,3,2,1,0:T(8,128)}, bf16[2,256,1152]{2,1,0:T(8,128)(2,1)}) custom-call(bf16[4,2,2,576,128]{4,3,2,1,0:T(8,128)(2,1)} %get-tuple-element.11.out_h, bf16[4,2,176,128]{3,2,1,0:T(8,128)(2,1)} %get-tuple-element.12.cot_h, ...), custom_call_target="tpu_custom_call" | custom-call | tf_op jit(solution)/shard_map/unpack/pallas_call | solution.py:832

commit v6 on v4

--- a/solution.py
+++ b/solution.py
@@ -640,7 +640,6 @@
                     @pl.when(f == 0)
                     def _():
                         leave(0, 0, True)
-                        leave(1, 0, True)
 
                 pb = {}
                 for w, (t, heads) in enumerate(windows):
@@ -711,7 +710,7 @@
 
         backward[0].spread()
         backward[1].spread()
-        leave(0, 1, True)
+        leave(1, 0, True)
         for f in range(2):
             leave(0, f, False)
             leave(1, f, False)
@@ -729,6 +728,7 @@
         backward[1].group_sums()
         backward[0].send_back()
         backward[1].send_back()
+        leave(0, 1, True)
         leave(1, 1, True)
         backward[0].pair_back()
         backward[0].finish()

time: 108 us -> 108 us (level)
  no operation moved by 1% of the time
where the time goes in v6:
time: 108 us
  Pallas kernels  107 us (99%)
    pallas_call x1, Pallas kernels, on_device(): pl.pallas_call(functools.partial(kernel, shape), out_shape=[jax.ShapeDtyp...  102 us
    pallas_call x1, Pallas kernels, unpacked(): pl.pallas_call(functools.partial(unpack_kernel, nsp), out_shape=[heads, h...  4.87 us

profile of v6, /device:TPU:1, one launch (start us, length us, event | category | flops | bytes accessed | tf_op | source)
XLA Modules:
  0.0 108.2 jit_solution(778169255579871873)
XLA Ops:
  0.6 102.5 %flow_layer.1 = (bf16[4,2,2,576,128]{4,3,2,1,0:T(8,128)(2,1)}, bf16[4,2,176,128]{3,2,1,0:T(8,128)(2,1)}, bf16[2,256,1152]{2,1,0:T(8,128)(2,1)}) custom-call(bf16[2,256,384]{2,1,0:T(8,128)(2,1)} %bitcast.11, bf16[9,1152,384]{2,1,0:T(8,128)(2,1)} %bitcast.8, bf16[384,1152]{1,0:T(8,128)(2,1)} %embed_h.1, bf16[1152,1152]{1,0:T(8,128)(2,1)} %q_h.1, ...), custom_call_target="tpu_custom_call" | custom-call | tf_op jit(solution)/shard_map/flow_layer/pallas_call | solution.py:865
  103.1 4.9 %unpack.1 = (bf16[2,4,256,288]{3,2,1,0:T(8,128)(2,1)}, bf16[2,4,256,288]{3,2,1,0:T(8,128)(2,1)}, f32[2,4,4,72,72]{4,3,2,1,0:T(8,128)}, bf16[2,256,1152]{2,1,0:T(8,128)(2,1)}) custom-call(bf16[4,2,2,576,128]{4,3,2,1,0:T(8,128)(2,1)} %get-tuple-element.11.out_h, bf16[4,2,176,128]{3,2,1,0:T(8,128)(2,1)} %get-tuple-element.12.cot_h, ...), custom_call_target="tpu_custom_call" | custom-call | tf_op jit(solution)/shard_map/unpack/pallas_call | solution.py:832
